TPU v7x, 512 devices: a whole 4x4x16 slice. The times are simulated.
512 devices in a mesh: row: 16 (over z_hi, y), col: 32 (over z_lo, x, core).
Axes of the slice: x: 4, y: 4, z: 16 (z_hi: 4, z_lo: 4; z = z_hi * 4 + z_lo), core: 2. Of those that a mesh axis runs over, the one named last changes fastest.
Arguments:
- inverse_block: bfloat16 [6144, 6144], P('row', 'col')
- panels: bfloat16 [2, 6144, 4096], P(None, 'row', 'col'), may hold values from -0.078125 to 0.078125
- structure: int32 [2, 48], replicated, may hold values 0 or 1
- pivot_inverse: bfloat16 [2, 4096, 4096], P(None, 'row', 'col')
Outputs:
- panel_inverse: bfloat16 [2, 6144, 4096], P(None, 'row', 'col')
- diagonal_inverse: bfloat16 [2, 4096, 4096], P(None, 'row', 'col')
All inputs are finite; a program needn't handle non-finite values.
Results may differ from a plain program's by a relative error of at most 0.019.
Values may be sent and summed in bfloat16 or wider, within the bound.
No kernel may reach another device: no remote copies, remote signals or barrier semaphores. Data moves between devices by JAX's collectives and lax.ppermute only.
A program may use at most 64 MiB of HBM per device.

v0:
```python
import jax
import jax.numpy as jnp
from jax import lax
from jax.sharding import PartitionSpec as P

SUPERNODES = 2
TILE = 128


def on_device(inverse_block, panels, structure, pivot_inverse):
    row_index = lax.axis_index("row")
    local_rows = panels.shape[1]
    tiles_here = local_rows // TILE
    tile_flags = lax.dynamic_slice_in_dim(structure, row_index * tiles_here, tiles_here, 1)
    row_flags = jnp.repeat(tile_flags, TILE, axis=1).astype(jnp.bfloat16)
    masked = panels * row_flags[:, :, None]
    all_rows = lax.all_gather(masked, "row", axis=1, tiled=True)
    product = jnp.einsum(
        "ik,skj->sij",
        lax.all_gather(inverse_block, "col", axis=1, tiled=True),
        all_rows,
        preferred_element_type=jnp.float32,
    )
    row_weight = row_flags.astype(jnp.float32)[:, :, None]
    panel_inverse = (-(product * row_weight)).astype(jnp.bfloat16)
    share_rows = pivot_inverse.shape[1]
    full_cols = lax.all_gather(masked, "col", axis=2, tiled=True)
    pieces = []
    for sup in range(SUPERNODES):

        def term(start, count, sup=sup):
            left_part = full_cols[sup]
            return jnp.einsum(
                "si,sj->ij", left_part, panel_inverse[sup], preferred_element_type=jnp.float32
            )

        pieces.append(
            lax.psum_scatter(
                term(jnp.int32(0), lax.axis_size("row") * share_rows).astype(jnp.bfloat16),
                "row",
                scatter_dimension=0,
                tiled=True,
            ).astype(jnp.float32)
        )
    summed = jnp.stack(pieces)
    diagonal_inverse = (pivot_inverse.astype(jnp.float32) - summed).astype(jnp.bfloat16)
    return (panel_inverse, diagonal_inverse)


def solution(mesh):
    in_specs = (P("row", "col"), P(None, "row", "col"), P(), P(None, "row", "col"))
    out_specs = (P(None, "row", "col"), P(None, "row", "col"))
    return jax.shard_map(
        on_device, mesh=mesh, in_specs=in_specs, out_specs=out_specs, check_vma=False
    )
```

profile of v0, /device:TPU:6, one launch (start us, length us, event | category | flops | bytes accessed | tf_op | source)
XLA Modules:
  0.0 512.6 jit_solution(7273178180423362731)
XLA Ops:
  7.2 0.0 all-gather.4.cloned.1.call-start
  7.2 0.8 dynamic-slice_convert_fusion
  8.0 0.1 broadcast_bitcast_fusion
  8.1 1.1 copy.8
  9.1 0.7 broadcast_multiply_fusion
  9.9 0.0 all-gather.4.cloned.1.call-update
  9.9 0.0 all-gather.6.cloned.1.call-start
  9.9 0.7 all-gather.6.cloned.1.call-update
  10.6 0.0 all-gather.8.cloned.1.call-start
  10.7 0.7 all-gather.8.cloned.1.call-update
  11.4 0.0 reduce-scatter.3.cloned.1.call-start
  11.4 125.5 %all-gather.4.cloned.1.call-done = bf16[2,6144,128]{1,2,0:T(8,128)(2,1)} async-done(((bf16[2,384,128]{1,2,0:T(8,128)(2,1)}), bf16[2,6144,128]{1,2,0:T(8,128)(2,1)}) %all-gather.4.cloned.1.call-update) | async-done | bytes 3145744 | tf_op jit(solution)/shard_map/all_gather | solution.py:17
  136.9 63.8 %all-gather.6.cloned.1.call-done = bf16[384,6144]{0,1:T(8,128)(2,1)} async-done(((bf16[384,192]{0,1:T(8,128)(2,1)}), bf16[384,6144]{0,1:T(8,128)(2,1)}) %all-gather.6.cloned.1.call-update) | async-done | bytes 4718608 | tf_op jit(solution)/shard_map/all_gather | solution.py:20
  200.7 5.1 fusion.11
  205.8 67.9 %all-gather.8.cloned.1.call-done = bf16[2,384,4096]{1,2,0:T(8,128)(2,1)} async-done(((bf16[2,384,128]{1,2,0:T(8,128)(2,1)}), bf16[2,384,4096]{1,2,0:T(8,128)(2,1)}) %all-gather.8.cloned.1.call-update) | async-done | bytes 6291472 | tf_op jit(solution)/shard_map/all_gather | solution.py:27
  273.6 3.9 convolution_convert_fusion.1
  277.5 0.0 reduce-scatter.3.cloned.1.call-update
  277.5 0.0 copy-start
  277.5 0.0 reduce-scatter.5.cloned.1.call-start
  277.6 3.9 convolution_convert_fusion
  281.5 0.0 reduce-scatter.5.cloned.1.call-update
  281.5 0.8 copy.9
  282.4 109.4 %reduce-scatter.3.cloned.1.call-done = bf16[256,128]{1,0:T(8,128)(2,1)} async-done(((bf16[4096,128]{1,0:T(8,128)(2,1)}), bf16[256,128]{1,0:T(8,128)(2,1)}) %reduce-scatter.3.cloned.1.call-update) | async-done | bytes 65552 | tf_op jit(solution)/shard_map/reduce_scatter | solution.py:38
  391.7 112.8 %reduce-scatter.5.cloned.1.call-done = bf16[256,128]{1,0:T(8,128)(2,1)} async-done(((bf16[4096,128]{1,0:T(8,128)(2,1)}), bf16[256,128]{1,0:T(8,128)(2,1)}) %reduce-scatter.5.cloned.1.call-update) | async-done | bytes 65552 | tf_op jit(solution)/shard_map/reduce_scatter | solution.py:38
  504.5 0.0 copy-done
  504.5 1.6 subtract_convert_fusion
  (1 shorter events, 0.0 us)
Async XLA Ops:
  7.2 129.7 %all-gather.4.cloned.1.call-start = ((), (), s32[]{:S(2)}) async-start(), calls=%async_computation.2 | async-start | bytes 3342336 | tf_op jit(solution)/shard_map/all_gather | solution.py:17
  9.9 190.8 %all-gather.6.cloned.1.call-start = ((), (), s32[]{:S(2)}) async-start(), calls=%async_computation.3 | async-start | bytes 4866048 | tf_op jit(solution)/shard_map/all_gather | solution.py:20
  10.6 263.0 %all-gather.8.cloned.1.call-start = ((), (), s32[]{:S(2)}) async-start(), calls=%async_computation.4 | async-start | bytes 6488064 | tf_op jit(solution)/shard_map/all_gather | solution.py:27
  11.4 380.4 %reduce-scatter.3.cloned.1.call-start = ((), (), s32[]{:S(2)}) async-start(), calls=%async_computation.5 | async-start | bytes 1114112 | tf_op jit(solution)/shard_map/reduce_scatter | solution.py:38
  277.5 227.0 %copy-start = (bf16[2,256,128]{2,1,0:T(8,128)(2,1)S(1)}, bf16[2,256,128]{2,1,0:T(8,128)(2,1)}, u32[]{:S(2)}) copy-start(bf16[2,256,128]{2,1,0:T(8,128)(2,1)} %param.7) | copy-start | bytes 393220
  277.5 227.0 %reduce-scatter.5.cloned.1.call-start = ((), (), s32[]{:S(2)}) async-start(), calls=%async_computation.6 | async-start | bytes 1114112 | tf_op jit(solution)/shard_map/reduce_scatter | solution.py:38
Sparse Core Ops, SparseCore 0:
  11.6 125.2 all-gather.3
  139.0 61.5 all-gather.5
  203.3 70.2 all-gather.7
  277.6 114.0 reduce-scatter.2
  396.2 108.2 reduce-scatter.4
where the time goes:
time: 513 us
  waiting for transfers between devices  481 us (94%)
  between operations  13.8 us (3%)
  matrix products  12.9 us (3%)
    reduce_scatter x2, waiting for transfers between devices, on_device(): lax.psum_scatter(term(jnp.int32(0), lax.axis_size('row') * share_rows).as...  222 us
    all_gather x1, waiting for transfers between devices, on_device(): all_rows = lax.all_gather(masked, 'row', axis=1, tiled=True)  125 us
    all_gather x1, waiting for transfers between devices, on_device(): full_cols = lax.all_gather(masked, 'col', axis=2, tiled=True)  67.9 us
    all_gather x1, waiting for transfers between devices, on_device(): lax.all_gather(inverse_block, 'col', axis=1, tiled=True)  63.8 us
  transfers between devices with their start and end apart: 5, of which 5 were waited for; matrix products, arithmetic and copies ran while one was open for 2% of the time, Pallas kernels for 0%

commit v1 on v0

v1 whole, which is shorter than its diff:
```python
import functools

import jax
import jax.numpy as jnp
from jax import lax
from jax.experimental import pallas as pl
from jax.experimental.pallas import tpu as pltpu
from jax.sharding import Mesh, PartitionSpec as P

SUPERNODES = 2
TILE = 128
AXES = ("zh", "y", "zl", "x", "core")
SIZES = (4, 4, 4, 4, 2)
CONTRACT_ROWS = (((0,), (0,)), ((), ()))


def device_index(zh, y, zl, x, core):
    return (((zh * 4 + y) * 4 + zl) * 4 + x) * 2 + core


def transpose_pairs():
    pairs = []
    for zh in range(4):
        for y in range(4):
            for zl in range(4):
                for x in range(4):
                    for core in range(2):
                        pairs.append((device_index(zh, y, zl, x, core), device_index(zh, x, zl, y, core)))
    return pairs


def panel_kernel(block_ref, rows_ref, weight_ref, out_ref, acc_ref):
    step = pl.program_id(0)

    @pl.when(step == 0)
    def _():
        acc_ref[...] = jnp.zeros_like(acc_ref)

    acc_ref[...] += lax.dot_general(
        block_ref[...], rows_ref[0, 0], CONTRACT_ROWS, preferred_element_type=jnp.float32
    )

    @pl.when(step == pl.num_programs(0) - 1)
    def _():
        out_ref[...] = (-(acc_ref[...] * weight_ref[...])).astype(out_ref.dtype)


def panel_product(block_t, rows, weight):
    depth, width = rows.shape[2:]
    out_rows = block_t.shape[1]
    return pl.pallas_call(
        panel_kernel,
        grid=(16,),
        in_specs=[
            pl.BlockSpec((depth, out_rows), lambda s: (s, 0)),
            pl.BlockSpec((1, 1, depth, width), lambda s: (s % 4, s // 4, 0, 0)),
            pl.BlockSpec((out_rows, width), lambda s: (0, 0)),
        ],
        out_specs=pl.BlockSpec((out_rows, width), lambda s: (0, 0)),
        out_shape=jax.ShapeDtypeStruct((out_rows, width), jnp.bfloat16),
        scratch_shapes=[pltpu.VMEM((out_rows, width), jnp.float32)],
        compiler_params=pltpu.CompilerParams(vmem_limit_bytes=32 * 1024 * 1024),
        cost_estimate=pl.CostEstimate(
            flops=2 * 16 * depth * out_rows * width, bytes_accessed=9 * 1024 * 1024, transcendentals=0
        ),
    )(block_t, rows, weight)


def diagonal_kernel(left_ref, right_ref, out_ref):
    for sup in range(SUPERNODES):
        cols = slice(sup * 128, sup * 128 + 128)
        total = jnp.zeros((128, 128), jnp.float32)
        for y in range(4):
            total += lax.dot_general(
                left_ref[0, y, 0, :, cols], right_ref[y, :, cols], CONTRACT_ROWS,
                preferred_element_type=jnp.float32,
            )
        out_ref[0, sup] = total.astype(out_ref.dtype)


def diagonal_partial(left, right):
    depth, width = right.shape[1:]
    return pl.pallas_call(
        diagonal_kernel,
        grid=(4, 2),
        in_specs=[
            pl.BlockSpec((1, 4, 1, depth, width), lambda a, c: (a, 0, c, 0, 0)),
            pl.BlockSpec((4, depth, width), lambda a, c: (0, 0, 0)),
        ],
        out_specs=pl.BlockSpec((1, SUPERNODES, 128, 128), lambda a, c: (a, 0, c, 0)),
        out_shape=jax.ShapeDtypeStruct((4, SUPERNODES, 256, 128), jnp.bfloat16),
        compiler_params=pltpu.CompilerParams(vmem_limit_bytes=32 * 1024 * 1024),
        cost_estimate=pl.CostEstimate(
            flops=2 * 1024 * 1536 * 256, bytes_accessed=8 * 1024 * 1024, transcendentals=0
        ),
    )(left, right)


def on_device(inverse_block, panels, structure, pivot_inverse):
    row_index = lax.axis_index("zh") * 4 + lax.axis_index("y")
    local_rows = panels.shape[1]
    tiles_here = local_rows // TILE
    tile_flags = lax.dynamic_slice_in_dim(structure, row_index * tiles_here, tiles_here, 1)
    row_flags = jnp.repeat(tile_flags, TILE, axis=1).astype(jnp.bfloat16)
    masked = panels * row_flags[:, :, None]
    wide = jnp.concatenate([masked[0], masked[1]], axis=1)
    weight = jnp.repeat(row_flags.astype(jnp.float32).T, 128, axis=1)

    block_t = lax.all_gather(inverse_block.T, ("zl", "x", "core"), axis=0, tiled=True)
    swapped = lax.ppermute(wide, AXES, transpose_pairs())
    columns = lax.all_gather(swapped, ("zl", "x", "core"), axis=0)
    columns = columns.reshape(4, 4, 2, local_rows, 256)

    rows = lax.all_gather(lax.all_gather(wide, "zh"), "y")
    panel = panel_product(block_t, rows, weight)
    panel_rows = lax.all_gather(panel, "y")
    partial = diagonal_partial(columns, panel_rows)
    shares = lax.all_to_all(partial, "zh", split_axis=0, concat_axis=0, tiled=True)
    summed = jnp.sum(shares.astype(jnp.float32), axis=0)
    diagonal_inverse = (pivot_inverse.astype(jnp.float32) - summed).astype(jnp.bfloat16)
    panel_inverse = jnp.stack([panel[:, :128], panel[:, 128:]])
    return (panel_inverse, diagonal_inverse)


def solution(mesh):
    fine = Mesh(mesh.devices.reshape(SIZES), AXES)
    row, col = ("zh", "y"), ("zl", "x", "core")
    in_specs = (P(row, col), P(None, row, col), P(), P(None, row, col))
    out_specs = (P(None, row, col), P(None, row, col))
    return jax.shard_map(
        on_device, mesh=fine, in_specs=in_specs, out_specs=out_specs, check_vma=False
    )
```

time: 513 us -> 299 us (0.58)
  the two profiles are of different devices: /device:TPU:6 before, /device:TPU:16 now
where the time goes in v1:
time: 299 us; the launch traced here: 298 us
  waiting for transfers between devices  192 us (64%)
  blocking collectives  55.4 us (19%)
  starting transfers between devices  15.7 us (5%)
  between operations  13.8 us (5%)
  Pallas kernels  9.94 us (3%)
  local copies, waits for them, and re-layouts  8.43 us (3%)
  other arithmetic  3.34 us (1%)
    all_gather x1, waiting for transfers between devices, on_device(): lax.all_gather(inverse_block.T, ('zl', 'x', 'core'), axis=0, tiled=True)  72.5 us
    all_gather x1, waiting for transfers between devices, on_device(): columns = lax.all_gather(swapped, ('zl', 'x', 'core'), axis=0)  51.1 us
    all_gather x1, blocking collectives, on_device(): rows = lax.all_gather(lax.all_gather(wide, 'zh'), 'y')  43 us
    all_to_all x1, waiting for transfers between devices, on_device(): lax.all_to_all(partial, 'zh', split_axis=0, concat_axis=0, tiled=True)  31.9 us
    all_gather x1, waiting for transfers between devices, on_device(): rows = lax.all_gather(lax.all_gather(wide, 'zh'), 'y')  28.4 us
    all_gather x1, blocking collectives, on_device(): panel_rows = lax.all_gather(panel, 'y')  12.4 us
    all_to_all x1, starting transfers between devices, on_device(): lax.all_to_all(partial, 'zh', split_axis=0, concat_axis=0, tiled=True)  10.9 us
    unnamed x12, local copies, waits for them, and re-layouts  7.79 us
  transfers between devices with their start and end apart: 5, of which 5 were waited for; matrix products, arithmetic and copies ran while one was open for 0% of the time, Pallas kernels for 2%

profile of v1, /device:TPU:16, one launch (start us, length us, event | category | flops | bytes accessed | tf_op | source)
XLA Modules:
  0.0 298.2 jit_solution(2916252618263115165)
XLA Ops:
  7.2 0.0 all-gather.10.cloned.1.call-start
  7.2 0.8 dynamic-slice_convert_fusion
  8.0 0.1 broadcast_bitcast_fusion
  8.1 1.1 broadcast_multiply_fusion
  9.2 43.0 %all-gather = bf16[1536,256]{1,0:T(8,128)(2,1)} all-gather(bf16[384,256]{1,0:T(8,128)(2,1)S(1)} %pad_maximum_fusion), channel_id=2, replica_groups=mesh['zh'=4,'y'=4,'zl'=4,'x'=4,'core'=2] {'zh'}, dimensions={0}, use_global_device_ids=true | all-gather | bytes 983040 | tf_op jit(solution)/shard_map/all_gather | solution.py:114
  52.2 0.0 all-gather.10.cloned.1.call-update
  52.2 0.0 all-gather.8.cloned.1.call-start
  52.3 0.7 all-gather.8.cloned.1.call-update
  53.0 0.0 all-gather.12.cloned.1.call-start
  53.0 4.7 %collective-permute-start = (bf16[384,256]{1,0:T(8,128)(2,1)S(1)}, bf16[384,256]{1,0:T(8,128)(2,1)S(1)}, u32[]{:S(2)}, u32[]{:S(2)}) collective-permute-start(bf16[384,256]{1,0:T(8,128)(2,1)S(1)} %pad_maximum_fusion), channel_id=1, source_target_pairs={{0,0},{1,1},{2,32},{3,33},{4,64},{5,65},{6,96},{7,97},{8,8},{9,9},... | collective-permute-start | bytes 589832 | tf_op jit(solution)/shard_map/ppermute | solution.py:110
  57.8 6.9 %collective-permute-done = bf16[384,256]{1,0:T(8,128)(2,1)S(1)} collective-permute-done((bf16[384,256]{1,0:T(8,128)(2,1)S(1)}, bf16[384,256]{1,0:T(8,128)(2,1)S(1)}, u32[]{:S(2)}, u32[]{:S(2)}) %collective-permute-start) | collective-permute-done | bytes 196640 | tf_op jit(solution)/shard_map/ppermute | solution.py:110
  64.6 0.0 copy-start.3
  64.6 0.7 copy-done.3
  65.3 0.0 all-gather.12.cloned.1.call-update
  65.3 0.1 copy.8
  65.5 0.5 broadcast_in_dim.8
  66.0 28.4 %all-gather.10.cloned.1.call-done = bf16[16,384,256]{2,1,0:T(8,128)(2,1)} async-done(((bf16[4,384,256]{2,1,0:T(8,128)(2,1)}), bf16[16,384,256]{2,1,0:T(8,128)(2,1)}) %all-gather.10.cloned.1.call-update) | async-done | bytes 3145744 | tf_op jit(solution)/shard_map/all_gather | solution.py:114
  94.4 72.5 %all-gather.8.cloned.1.call-done.block_ref = bf16[6144,384]{1,0:T(8,128)(2,1)} async-done(((bf16[192,384]{1,0:T(8,128)(2,1)}), bf16[6144,384]{1,0:T(8,128)(2,1)}) %all-gather.8.cloned.1.call-update) | async-done | bytes 4718608 | tf_op jit(solution)/shard_map/all_gather | solution.py:109
  166.9 0.0 copy-start.1
  166.9 2.3 copy-done.1
  169.3 1.9 copy-done.2
  171.2 5.1 %shard_map.59 = bf16[384,256]{1,0:T(8,128)(2,1)S(1)} custom-call(bf16[6144,384]{1,0:T(8,128)(2,1)S(1)} %copy-done.1, bf16[4,4,384,256]{3,2,1,0:T(8,128)(2,1)S(1)} %bitcast.25, f32[384,256]{1,0:T(8,128)S(1)} %bitcast.27), custom_call_target="tpu_custom_call" | custom-call | flops 1207959552 | bytes 9437184 | tf_op jit(solution)/shard_map/pallas_call | solution.py:51
  176.3 12.4 %all-gather.3 = bf16[1536,256]{1,0:T(8,128)(2,1)S(1)} all-gather(bf16[384,256]{1,0:T(8,128)(2,1)S(1)} %shard_map.59), channel_id=5, replica_groups=mesh['zh'=4,'y'=4,'zl'=4,'x'=4,'core'=2] {'y'}, dimensions={0}, use_global_device_ids=true | all-gather | bytes 983040 | tf_op jit(solution)/shard_map/all_gather | solution.py:116
  188.7 51.1 %all-gather.12.cloned.1.call-done = bf16[12288,256]{1,0:T(8,128)(2,1)} async-done(((bf16[384,256]{1,0:T(8,128)(2,1)}), bf16[12288,256]{1,0:T(8,128)(2,1)}) %all-gather.12.cloned.1.call-update) | async-done | bytes 6291472 | tf_op jit(solution)/shard_map/all_gather | solution.py:111
  239.8 2.8 copy-done
  242.6 4.8 %shard_map.60 = bf16[4,2,256,128]{3,2,1,0:T(8,128)(2,1)} custom-call(bf16[4,4,2,384,256]{4,3,2,1,0:T(8,128)(2,1)S(1)} %bitcast.24, bf16[4,384,256]{2,1,0:T(8,128)(2,1)S(1)} %bitcast.26), custom_call_target="tpu_custom_call" | custom-call | flops 805306368 | bytes 8388608 | tf_op jit(solution)/shard_map/pallas_call | solution.py:83
  247.4 10.9 %all-to-all-start = ((bf16[4,2,256,128]{3,2,1,0:T(8,128)(2,1)}), bf16[4,2,256,128]{3,2,1,0:T(8,128)(2,1)S(1)}, u32[]{:S(2)}, u32[]{:S(2)}) async-start(bf16[4,2,256,128]{3,2,1,0:T(8,128)(2,1)} %shard_map.60), calls=%async_computation | async-start | bytes 1048576 | tf_op jit(solution)/shard_map/all_to_all | solution.py:118
  258.3 0.7 pad_maximum_fusion.1
  259.0 31.9 %all-to-all-done = bf16[4,2,256,128]{3,2,1,0:T(8,128)(2,1)S(1)} async-done(((bf16[4,2,256,128]{3,2,1,0:T(8,128)(2,1)}), bf16[4,2,256,128]{3,2,1,0:T(8,128)(2,1)S(1)}, u32[]{:S(2)}, u32[]{:S(2)}) %all-to-all-start) | async-done | bytes 524320 | tf_op jit(solution)/shard_map/all_to_all | solution.py:118
  290.9 0.1 convert_reduce_fusion
  291.0 0.0 copy-done.4
  291.0 0.7 subtract_convert_fusion
  (8 shorter events, 0.1 us)
Async XLA Ops:
  7.2 87.2 %all-gather.10.cloned.1.call-start = ((), (), s32[]{:S(2)}) async-start(), calls=%async_computation.2 | async-start | bytes 3932160 | tf_op jit(solution)/shard_map/all_gather | solution.py:114
  52.2 114.7 %all-gather.8.cloned.1.call-start = ((), (), s32[]{:S(2)}) async-start(), calls=%async_computation.1 | async-start | bytes 4866048 | tf_op jit(solution)/shard_map/all_gather | solution.py:109
  53.0 186.8 %all-gather.12.cloned.1.call-start = ((), (), s32[]{:S(2)}) async-start(), calls=%async_computation.3 | async-start | bytes 6488064 | tf_op jit(solution)/shard_map/all_gather | solution.py:111
  53.0 11.6 %collective-permute-start = (bf16[384,256]{1,0:T(8,128)(2,1)S(1)}, bf16[384,256]{1,0:T(8,128)(2,1)S(1)}, u32[]{:S(2)}, u32[]{:S(2)}) collective-permute-start(bf16[384,256]{1,0:T(8,128)(2,1)S(1)} %pad_maximum_fusion), channel_id=1, source_target_pairs={{0,0},{1,1},{2,32},{3,33},{4,64},{5,65},{6,96},{7,97},{8,8},{9,9},... | collective-permute-start | bytes 589832 | tf_op jit(solution)/shard_map/ppermute | solution.py:110
  64.6 0.7 copy-start.3
  166.9 2.3 copy-start.1
  169.3 1.9 copy-start.2
  239.8 2.8 copy-start
  242.6 48.3 %copy-start.4 = (bf16[2,256,128]{2,1,0:T(8,128)(2,1)S(1)}, bf16[2,256,128]{2,1,0:T(8,128)(2,1)}, u32[]{:S(2)}) copy-start(bf16[2,256,128]{2,1,0:T(8,128)(2,1)} %param.7) | copy-start | bytes 393220
  247.4 43.5 %all-to-all-start = ((bf16[4,2,256,128]{3,2,1,0:T(8,128)(2,1)}), bf16[4,2,256,128]{3,2,1,0:T(8,128)(2,1)S(1)}, u32[]{:S(2)}, u32[]{:S(2)}) async-start(bf16[4,2,256,128]{3,2,1,0:T(8,128)(2,1)} %shard_map.60), calls=%async_computation | async-start | bytes 1048576 | tf_op jit(solution)/shard_map/all_to_all | solution.py:118
Sparse Core Ops, SparseCore 0:
  52.4 41.9 all-gather.9
  96.5 70.3 all-gather.7
  169.7 70.1 all-gather.11

commit v2 on v0

v2 whole, which is shorter than its diff:
```python
import jax
import jax.numpy as jnp
from jax import lax
from jax.experimental import pallas as pl
from jax.experimental.pallas import tpu as pltpu
from jax.sharding import Mesh, PartitionSpec as P

SUPERNODES = 2
TILE = 128
AXES = ("zh", "y", "zl", "x", "core")
SIZES = (4, 4, 4, 4, 2)
CONTRACT_ROWS = (((0,), (0,)), ((), ()))
VMEM_BYTES = 40 * 1024 * 1024


def pairs(move):
    listed = []
    for zh in range(4):
        for y in range(4):
            for zl in range(4):
                for x in range(4):
                    for core in range(2):
                        place = []
                        for at in ((zh, y, zl, x, core), move(zh, y, zl, x, core)):
                            index = 0
                            for size, coordinate in zip(SIZES, at):
                                index = index * size + coordinate
                            place.append(index)
                        listed.append(tuple(place))
    return listed


SWAP_CORES = pairs(lambda zh, y, zl, x, core: (zh, y, zl, x, 1 - core))
TURN = pairs(lambda zh, y, zl, x, core: (zh, x, zl, y, core))


def move(value, listed):
    return lax.ppermute(value, AXES, listed)


def panel_kernel(core_ref, own_ref, other_ref, rows_ref, out_ref):
    half = own_ref.shape[2]
    core = core_ref[0]
    total = jnp.zeros(out_ref.shape[1:], jnp.float32)
    for group in range(4):
        for block, part in ((own_ref, core), (other_ref, 1 - core)):
            start = pl.multiple_of(part * half, half)
            total += lax.dot_general(
                block[0, group], rows_ref[group, pl.ds(start, half), :], CONTRACT_ROWS,
                preferred_element_type=jnp.float32,
            )
    out_ref[0] = total.astype(out_ref.dtype)


def panel_partial(core, own, other, rows):
    groups, steps, half, height = own.shape
    width = rows.shape[2]
    block = pl.BlockSpec((1, steps, half, height), lambda g, core: (g, 0, 0, 0))
    return pl.pallas_call(
        panel_kernel,
        grid_spec=pltpu.PrefetchScalarGridSpec(
            num_scalar_prefetch=1,
            grid=(groups,),
            in_specs=[block, block, pl.BlockSpec(rows.shape, lambda g, core: (0, 0, 0))],
            out_specs=pl.BlockSpec((1, height, width), lambda g, core: (g, 0, 0)),
        ),
        out_shape=jax.ShapeDtypeStruct((groups, height, width), jnp.bfloat16),
        compiler_params=pltpu.CompilerParams(vmem_limit_bytes=VMEM_BYTES),
        cost_estimate=pl.CostEstimate(
            flops=4 * groups * steps * half * height * width,
            bytes_accessed=7 * 1024 * 1024,
            transcendentals=0,
        ),
    )(core, own, other, rows)


def diagonal_kernel(left_ref, right_ref, out_ref):
    total = jnp.zeros((left_ref.shape[3], right_ref.shape[2]), jnp.float32)
    for y in range(4):
        total += lax.dot_general(
            left_ref[y, 0], right_ref[y], CONTRACT_ROWS, preferred_element_type=jnp.float32
        )
    value = total.astype(out_ref.dtype)
    out_ref[0, 0] = value[:, :128]
    out_ref[0, 1] = value[:, 128:]


def diagonal_partial(left, right):
    groups, steps, depth, width = left.shape
    return pl.pallas_call(
        diagonal_kernel,
        grid=(steps,),
        in_specs=[
            pl.BlockSpec((groups, 1, depth, width), lambda g: (0, g, 0, 0)),
            pl.BlockSpec(right.shape, lambda g: (0, 0, 0)),
        ],
        out_specs=pl.BlockSpec((1, 2, width, 128), lambda g: (g, 0, 0, 0)),
        out_shape=jax.ShapeDtypeStruct((4, 2, width, 128), jnp.bfloat16),
        compiler_params=pltpu.CompilerParams(vmem_limit_bytes=VMEM_BYTES),
        cost_estimate=pl.CostEstimate(
            flops=2 * groups * steps * depth * width * 256,
            bytes_accessed=5 * 1024 * 1024,
            transcendentals=0,
        ),
    )(left, right)


def on_device(inverse_block, panels, structure, pivot_inverse):
    core = lax.axis_index("core")
    first = core == 0
    row_index = lax.axis_index("zh") * 4 + lax.axis_index("y")
    local_rows = panels.shape[1]
    tiles_here = local_rows // TILE
    tile_flags = lax.dynamic_slice_in_dim(structure, row_index * tiles_here, tiles_here, 1)
    row_flags = jnp.repeat(tile_flags, TILE, axis=1).astype(jnp.bfloat16)
    masked = panels * row_flags[:, :, None]
    weight = jnp.where(first, row_flags[0], row_flags[1]).astype(jnp.float32)[:, None]

    def swap_halves(mine, theirs):
        got = move(theirs, SWAP_CORES)
        return jnp.where(first, mine, got), jnp.where(first, got, mine)

    wide = jnp.concatenate(
        swap_halves(jnp.where(first, masked[0], masked[1]), jnp.where(first, masked[1], masked[0])), axis=1
    )
    turned_block = move(inverse_block.T, TURN)
    turned_panel = move(wide, TURN)
    block_parts = lax.all_gather(turned_block, "zl")
    own = lax.all_gather(block_parts, "x")
    turned_panel, block_parts = lax.optimization_barrier((turned_panel, block_parts))
    panel_parts = lax.all_gather(turned_panel, "zl")
    columns = lax.all_gather(panel_parts, "x")
    wide, panel_parts = lax.optimization_barrier((wide, panel_parts))
    rows = lax.all_gather(wide, "zh")
    own, rows = lax.optimization_barrier((own, rows))
    other = move(own, SWAP_CORES)

    partial = panel_partial(jnp.reshape(core, (1,)).astype(jnp.int32), own, other, rows)
    parts = lax.all_to_all(partial, "y", split_axis=0, concat_axis=0, tiled=True)
    panel = (-(jnp.sum(parts.astype(jnp.float32), axis=0) * weight)).astype(jnp.bfloat16)
    panel_rows = lax.all_gather(panel, "y")
    left, right = panel[:, :128], panel[:, 128:]
    panel_inverse = jnp.stack(
        swap_halves(jnp.where(first, left, right), jnp.where(first, right, left))
    )

    shares = diagonal_partial(columns, panel_rows).reshape(8, 256, 128)
    shares = lax.all_to_all(shares, ("zh", "core"), split_axis=0, concat_axis=0, tiled=True)
    summed = jnp.sum(shares.reshape(4, 2, 256, 128).astype(jnp.float32), axis=0)
    diagonal_inverse = (pivot_inverse.astype(jnp.float32) - summed).astype(jnp.bfloat16)
    return (panel_inverse, diagonal_inverse)


def solution(mesh):
    fine = Mesh(mesh.devices.reshape(SIZES), AXES)
    row, col = ("zh", "y"), ("zl", "x", "core")
    in_specs = (P(row, col), P(None, row, col), P(), P(None, row, col))
    out_specs = (P(None, row, col), P(None, row, col))
    return jax.shard_map(
        on_device, mesh=fine, in_specs=in_specs, out_specs=out_specs, check_vma=False
    )
```

time: 513 us -> 213 us (0.42)
  waiting for transfers between devices: 481 us -> 68.2 us
  blocking collectives: 0 us -> 89.7 us
  starting transfers between devices: 0.2 us -> 27.1 us
  matrix products: 12.9 us -> 0 us
  Pallas kernels: 0 us -> 6.23 us
    all_gather x3 -> x2, waiting for transfers between devices: 257 us -> 0.01 us  [the longest x1 0.01 us: on_device(): own = lax.all_gather(block_parts, 'x')]
    reduce_scatter x2 -> x0, waiting for transfers between devices: 222 us -> none  [on_device(): lax.psum_scatter(term(jnp.int32(0), lax.axis_size('row') * share_rows).as...]
    all_gather x0 -> x4, blocking collectives: none -> 89.7 us  [the longest x1 37.4 us: on_device(): rows = lax.all_gather(wide, 'zh')]
    all_to_all x0 -> x2, waiting for transfers between devices: none -> 41.3 us  [the longest x1 28.5 us: on_device(): lax.all_to_all(shares, ('zh', 'core'), split_axis=0, concat_axis=0, tiled...]
    ppermute x0 -> x5, waiting for transfers between devices: none -> 26.9 us  [move(): return lax.ppermute(value, AXES, listed)]
    ppermute x0 -> x5, starting transfers between devices: none -> 16.7 us  [move(): return lax.ppermute(value, AXES, listed)]
    dot_general x3 -> x0, matrix products: 12.9 us -> none  [the longest x2 7.78 us: term(): jnp.einsum('si,sj->ij', left_part, panel_inverse[sup], preferred_element_...]
    all_to_all x0 -> x2, starting transfers between devices: none -> 10.3 us  [the longest x1 6.8 us: on_device(): lax.all_to_all(shares, ('zh', 'core'), split_axis=0, concat_axis=0, tiled...]
  transfers between devices with their start and end apart: 5 -> 9, of which waited for: 5 -> 7; matrix products, arithmetic and copies ran while one was open for 2% -> 1% of each run, Pallas kernels for 0% -> 2%
where the time goes in v2:
time: 213 us
  blocking collectives  89.7 us (42%)
  waiting for transfers between devices  68.2 us (32%)
  starting transfers between devices  27.1 us (13%)
  between operations  14.2 us (7%)
  Pallas kernels  6.23 us (3%)
  other arithmetic  3.74 us (2%)
  local copies, waits for them, and re-layouts  3.71 us (2%)
    all_gather x1, blocking collectives, on_device(): rows = lax.all_gather(wide, 'zh')  37.4 us
    all_to_all x1, waiting for transfers between devices, on_device(): lax.all_to_all(shares, ('zh', 'core'), split_axis=0, concat_axis=0, tiled...  28.5 us
    ppermute x5, waiting for transfers between devices, move(): return lax.ppermute(value, AXES, listed)  26.9 us
    all_gather x1, blocking collectives, on_device(): panel_parts = lax.all_gather(turned_panel, 'zl')  20.9 us
    all_gather x1, blocking collectives, on_device(): block_parts = lax.all_gather(turned_block, 'zl')  17.1 us
    ppermute x5, starting transfers between devices, move(): return lax.ppermute(value, AXES, listed)  16.7 us
    all_gather x1, blocking collectives, on_device(): panel_rows = lax.all_gather(panel, 'y')  14.3 us
    all_to_all x1, waiting for transfers between devices, on_device(): lax.all_to_all(partial, 'y', split_axis=0, concat_axis=0, tiled=True)  12.7 us
  transfers between devices with their start and end apart: 9, of which 7 were waited for; matrix products, arithmetic and copies ran while one was open for 1% of the time, Pallas kernels for 2%

profile of v2, /device:TPU:6, one launch (start us, length us, event | category | flops | bytes accessed | tf_op | source)
XLA Modules:
  0.0 212.9 jit_solution(12347025084330883156)
XLA Ops:
  7.2 4.8 %collective-permute-start = (bf16[192,384]{1,0:T(8,128)(2,1)}, bf16[192,384]{1,0:T(8,128)(2,1)S(1)}, u32[]{:S(2)}, u32[]{:S(2)}) collective-permute-start(bf16[192,384]{1,0:T(8,128)(2,1)} %bitcast.45), channel_id=1, source_target_pairs={{0,0},{1,1},{2,32},{3,33},{4,64},{5,65},{6,96},{7,97},{8,8},{9,9},... | collective-permute-start | bytes 442376 | tf_op jit(solution)/shard_map/ppermute | solution.py:38
  12.1 9.3 %collective-permute-done = bf16[192,384]{1,0:T(8,128)(2,1)S(1)} collective-permute-done((bf16[192,384]{1,0:T(8,128)(2,1)}, bf16[192,384]{1,0:T(8,128)(2,1)S(1)}, u32[]{:S(2)}, u32[]{:S(2)}) %collective-permute-start) | collective-permute-done | bytes 147488 | tf_op jit(solution)/shard_map/ppermute | solution.py:38
  21.4 17.1 %all-gather = bf16[768,384]{1,0:T(8,128)(2,1)} all-gather(bf16[192,384]{1,0:T(8,128)(2,1)S(1)} %collective-permute-done), channel_id=2, replica_groups=mesh['zh'=4,'y'=4,'zl'=4,'x'=4,'core'=2] {'zl'}, dimensions={0}, use_global_device_ids=true | all-gather | bytes 737280 | tf_op jit(solution)/shard_map/all_gather | solution.py:128
  38.6 0.8 dynamic-slice_convert_fusion
  39.3 0.1 broadcast_bitcast_fusion.1
  39.4 1.1 broadcast_multiply_fusion
  40.5 1.9 collective-permute-start.1
  42.4 1.3 collective-permute-done.1
  43.8 5.6 %collective-permute-start.2 = (bf16[384,256]{1,0:T(8,128)(2,1)S(1)}, bf16[384,256]{1,0:T(8,128)(2,1)S(1)}, u32[]{:S(2)}, u32[]{:S(2)}) collective-permute-start(bf16[384,256]{1,0:T(8,128)(2,1)S(1)} %pad_maximum_fusion), channel_id=1, source_target_pairs={{0,0},{1,1},{2,32},{3,33},{4,64},{5,65},{6,96},{7,97},{8,8},{9,9},... | collective-permute-start | bytes 589832 | tf_op jit(solution)/shard_map/ppermute | solution.py:38
  49.4 10.7 %collective-permute-done.2 = bf16[384,256]{1,0:T(8,128)(2,1)S(1)} collective-permute-done((bf16[384,256]{1,0:T(8,128)(2,1)S(1)}, bf16[384,256]{1,0:T(8,128)(2,1)S(1)}, u32[]{:S(2)}, u32[]{:S(2)}) %collective-permute-start.2) | collective-permute-done | bytes 196640 | tf_op jit(solution)/shard_map/ppermute | solution.py:38
  60.1 20.9 %all-gather.2 = bf16[1536,256]{1,0:T(8,128)(2,1)} all-gather(bf16[384,256]{1,0:T(8,128)(2,1)S(1)} %collective-permute-done.2), channel_id=4, replica_groups=mesh['zh'=4,'y'=4,'zl'=4,'x'=4,'core'=2] {'zl'}, dimensions={0}, use_global_device_ids=true | all-gather | bytes 983040 | tf_op jit(solution)/shard_map/all_gather | solution.py:131
  81.0 37.4 %all-gather.3 = bf16[1536,256]{1,0:T(8,128)(2,1)S(1)} all-gather(bf16[384,256]{1,0:T(8,128)(2,1)S(1)} %pad_maximum_fusion), channel_id=5, replica_groups=mesh['zh'=4,'y'=4,'zl'=4,'x'=4,'core'=2] {'zh'}, dimensions={0}, use_global_device_ids=true | all-gather | bytes 983040 | tf_op jit(solution)/shard_map/all_gather | solution.py:134
  118.4 1.9 collective-permute-start.3
  120.3 4.7 %collective-permute-done.3.other_ref = bf16[4,4,192,384]{3,2,1,0:T(8,128)(2,1)S(1)} collective-permute-done((bf16[4,4,192,384]{3,2,1,0:T(8,128)(2,1)}, bf16[4,4,192,384]{3,2,1,0:T(8,128)(2,1)S(1)}, u32[]{:S(2)}, u32[]{:S(2)}) %collective-permute-start.3) | collective-permute-done | bytes 2359328 | tf_op jit(solution)/shard_map/ppermute | solution.py:38
  125.0 1.7 copy-done.1
  126.7 3.3 %shard_map.59 = bf16[4,384,256]{2,1,0:T(8,128)(2,1)} custom-call(s32[1]{0:T(128)} %bitcast.core_ref, bf16[4,4,192,384]{3,2,1,0:T(8,128)(2,1)S(1)} %bitcast.40, bf16[4,4,192,384]{3,2,1,0:T(8,128)(2,1)S(1)} %collective-permute-done.3.other_ref, bf16[4,384,256]{2,1,0:T(8,128)(2,1)S(1)} %bitcast.37), custom_call_target="tpu_custom_call" | custom-call | flops 1207959552 | bytes 7340032 | tf_op jit(solution)/shard_map/pallas_call | solution.py:59
  130.0 3.5 %all-to-all-start = ((bf16[4,384,256]{2,1,0:T(8,128)(2,1)}), bf16[4,384,256]{2,1,0:T(8,128)(2,1)S(1)}, u32[]{:S(2)}, u32[]{:S(2)}) async-start(bf16[4,384,256]{2,1,0:T(8,128)(2,1)} %shard_map.59), calls=%async_computation | async-start | bytes 1572864 | tf_op jit(solution)/shard_map/all_to_all | solution.py:139
  133.5 0.1 broadcast_bitcast_fusion
  133.6 12.7 %all-to-all-done = bf16[4,384,256]{2,1,0:T(8,128)(2,1)S(1)} async-done(((bf16[4,384,256]{2,1,0:T(8,128)(2,1)}), bf16[4,384,256]{2,1,0:T(8,128)(2,1)S(1)}, u32[]{:S(2)}, u32[]{:S(2)}) %all-to-all-start) | async-done | bytes 786464 | tf_op jit(solution)/shard_map/all_to_all | solution.py:139
  146.4 0.1 convert_reduce_fusion
  146.5 0.1 fusion.1
  146.6 14.3 %all_gather.44.right_ref = bf16[4,384,256]{2,1,0:T(8,128)(2,1)S(1)} all-gather(bf16[1,384,256]{2,1,0:T(8,128)(2,1)S(1)} %fusion.1), channel_id=1, replica_groups=mesh['zh'=4,'y'=4,'zl'=4,'x'=4,'core'=2] {'y'}, dimensions={0}, use_global_device_ids=true | all-gather | bytes 983040 | tf_op jit(solution)/shard_map/all_gather | solution.py:141
  160.9 1.9 copy-done
  162.8 2.9 %shard_map.60 = bf16[4,2,256,128]{3,2,1,0:T(8,128)(2,1)} custom-call(bf16[4,4,384,256]{3,2,1,0:T(8,128)(2,1)S(1)} %bitcast.38, bf16[4,384,256]{2,1,0:T(8,128)(2,1)S(1)} %all_gather.44.right_ref), custom_call_target="tpu_custom_call" | custom-call | flops 805306368 | bytes 5242880 | tf_op jit(solution)/shard_map/pallas_call | solution.py:90
  165.7 6.8 %all-to-all-start.1 = ((bf16[8,256,128]{2,1,0:T(8,128)(2,1)}), bf16[8,256,128]{2,1,0:T(8,128)(2,1)S(1)}, u32[]{:S(2)}, u32[]{:S(2)}) async-start(bf16[8,256,128]{2,1,0:T(8,128)(2,1)} %bitcast.14), calls=%async_computation.1 | async-start | bytes 1048576 | tf_op jit(solution)/shard_map/all_to_all | solution.py:148
  172.5 0.1 negate_convert_fusion
  172.7 2.4 %collective-permute-start.4 = (bf16[384,128]{1,0:T(8,128)(2,1)S(1)}, bf16[384,128]{1,0:T(8,128)(2,1)S(1)}, u32[]{:S(2)}, u32[]{:S(2)}) collective-permute-start(bf16[384,128]{1,0:T(8,128)(2,1)S(1)} %broadcast_select_fusion.1), channel_id=1, source_target_pairs={{0,1},{1,0},{2,3},{3,2},{4,5},{5,4},{6,7},{7,6},{8,9},{9,8},{10,11... | collective-permute-start | bytes 294920 | tf_op jit(solution)/shard_map/ppermute | solution.py:38
  175.1 0.9 collective-permute-done.4
  176.0 0.7 pad_maximum_fusion.1
  176.7 28.5 %all-to-all-done.1 = bf16[8,256,128]{2,1,0:T(8,128)(2,1)S(1)} async-done(((bf16[8,256,128]{2,1,0:T(8,128)(2,1)}), bf16[8,256,128]{2,1,0:T(8,128)(2,1)S(1)}, u32[]{:S(2)}, u32[]{:S(2)}) %all-to-all-start.1) | async-done | bytes 524320 | tf_op jit(solution)/shard_map/all_to_all | solution.py:148
  205.3 0.1 convert_reduce_fusion.1
  205.3 0.7 subtract_convert_fusion
  (17 shorter events, 0.2 us)
Async XLA Ops:
  7.2 111.3 %all-gather.8.cloned.1.call-start = ((), (), s32[]{:S(2)}) async-start(), calls=%async_computation.2 | async-start | bytes 2949120 | tf_op jit(solution)/shard_map/all_gather | solution.py:129
  7.2 14.2 %collective-permute-start = (bf16[192,384]{1,0:T(8,128)(2,1)}, bf16[192,384]{1,0:T(8,128)(2,1)S(1)}, u32[]{:S(2)}, u32[]{:S(2)}) collective-permute-start(bf16[192,384]{1,0:T(8,128)(2,1)} %bitcast.45), channel_id=1, source_target_pairs={{0,0},{1,1},{2,32},{3,33},{4,64},{5,65},{6,96},{7,97},{8,8},{9,9},... | collective-permute-start | bytes 442376 | tf_op jit(solution)/shard_map/ppermute | solution.py:38
  38.5 122.4 %all-gather.10.cloned.1.call-start = ((), (), s32[]{:S(2)}) async-start(), calls=%async_computation.3 | async-start | bytes 3932160 | tf_op jit(solution)/shard_map/all_gather | solution.py:132
  40.5 3.2 %collective-permute-start.1 = (bf16[384,128]{1,0:T(8,128)(2,1)S(1)}, bf16[384,128]{1,0:T(8,128)(2,1)S(1)}, u32[]{:S(2)}, u32[]{:S(2)}) collective-permute-start(bf16[384,128]{1,0:T(8,128)(2,1)S(1)} %select_bitcast_fusion.2), channel_id=1, source_target_pairs={{0,1},{1,0},{2,3},{3,2},{4,5},{5,4},{6,7},{7,6},{8,9},{9,8},{10,11... | collective-permute-start | bytes 294920 | tf_op jit(solution)/shard_map/ppermute | solution.py:38
  43.8 16.3 %collective-permute-start.2 = (bf16[384,256]{1,0:T(8,128)(2,1)S(1)}, bf16[384,256]{1,0:T(8,128)(2,1)S(1)}, u32[]{:S(2)}, u32[]{:S(2)}) collective-permute-start(bf16[384,256]{1,0:T(8,128)(2,1)S(1)} %pad_maximum_fusion), channel_id=1, source_target_pairs={{0,0},{1,1},{2,32},{3,33},{4,64},{5,65},{6,96},{7,97},{8,8},{9,9},... | collective-permute-start | bytes 589832 | tf_op jit(solution)/shard_map/ppermute | solution.py:38
  118.4 6.6 %collective-permute-start.3 = (bf16[4,4,192,384]{3,2,1,0:T(8,128)(2,1)}, bf16[4,4,192,384]{3,2,1,0:T(8,128)(2,1)S(1)}, u32[]{:S(2)}, u32[]{:S(2)}) collective-permute-start(bf16[4,4,192,384]{3,2,1,0:T(8,128)(2,1)} %bitcast.39), channel_id=1, source_target_pairs={{0,1},{1,0},{2,3},{3,2},{4,5},{5,4},{6,7},{7,6},{8,9},{9,8},{10,11... | collective-permute-start | bytes 7077896 | tf_op jit(solution)/shard_map/ppermute | solution.py:38
  125.0 1.7 copy-start.1
  130.0 16.3 %all-to-all-start = ((bf16[4,384,256]{2,1,0:T(8,128)(2,1)}), bf16[4,384,256]{2,1,0:T(8,128)(2,1)S(1)}, u32[]{:S(2)}, u32[]{:S(2)}) async-start(bf16[4,384,256]{2,1,0:T(8,128)(2,1)} %shard_map.59), calls=%async_computation | async-start | bytes 1572864 | tf_op jit(solution)/shard_map/all_to_all | solution.py:139
  160.9 1.9 copy-start
  165.7 39.6 %copy-start.2 = (bf16[2,256,128]{2,1,0:T(8,128)(2,1)S(1)}, bf16[2,256,128]{2,1,0:T(8,128)(2,1)}, u32[]{:S(2)}) copy-start(bf16[2,256,128]{2,1,0:T(8,128)(2,1)} %param.7) | copy-start | bytes 393220
  165.7 39.5 %all-to-all-start.1 = ((bf16[8,256,128]{2,1,0:T(8,128)(2,1)}), bf16[8,256,128]{2,1,0:T(8,128)(2,1)S(1)}, u32[]{:S(2)}, u32[]{:S(2)}) async-start(bf16[8,256,128]{2,1,0:T(8,128)(2,1)} %bitcast.14), calls=%async_computation.1 | async-start | bytes 1048576 | tf_op jit(solution)/shard_map/all_to_all | solution.py:148
  172.7 3.3 %collective-permute-start.4 = (bf16[384,128]{1,0:T(8,128)(2,1)S(1)}, bf16[384,128]{1,0:T(8,128)(2,1)S(1)}, u32[]{:S(2)}, u32[]{:S(2)}) collective-permute-start(bf16[384,128]{1,0:T(8,128)(2,1)S(1)} %broadcast_select_fusion.1), channel_id=1, source_target_pairs={{0,1},{1,0},{2,3},{3,2},{4,5},{5,4},{6,7},{7,6},{8,9},{9,8},{10,11... | collective-permute-start | bytes 294920 | tf_op jit(solution)/shard_map/ppermute | solution.py:38
Sparse Core Ops, SparseCore 0:
  38.6 40.6 all-gather.7
  81.4 47.3 all-gather.9

commit v3 on v2

--- a/solution.py
+++ b/solution.py
@@ -10,7 +10,7 @@
 AXES = ("zh", "y", "zl", "x", "core")
 SIZES = (4, 4, 4, 4, 2)
 CONTRACT_ROWS = (((0,), (0,)), ((), ()))
-VMEM_BYTES = 40 * 1024 * 1024
+VMEM_BYTES = 60 * 1024 * 1024
 
 
 def pairs(move):
@@ -38,32 +38,29 @@
     return lax.ppermute(value, AXES, listed)
 
 
-def panel_kernel(core_ref, own_ref, other_ref, rows_ref, out_ref):
-    half = own_ref.shape[2]
-    core = core_ref[0]
+def panel_kernel(block_ref, rows_ref, out_ref):
+    half = block_ref.shape[3]
     total = jnp.zeros(out_ref.shape[1:], jnp.float32)
     for group in range(4):
-        for block, part in ((own_ref, core), (other_ref, 1 - core)):
-            start = pl.multiple_of(part * half, half)
+        for part in range(2):
             total += lax.dot_general(
-                block[0, group], rows_ref[group, pl.ds(start, half), :], CONTRACT_ROWS,
-                preferred_element_type=jnp.float32,
+                block_ref[0, part, group], rows_ref[group, part * half : part * half + half, :],
+                CONTRACT_ROWS, preferred_element_type=jnp.float32,
             )
     out_ref[0] = total.astype(out_ref.dtype)
 
 
-def panel_partial(core, own, other, rows):
-    groups, steps, half, height = own.shape
+def panel_partial(block, rows):
+    groups, parts, steps, half, height = block.shape
     width = rows.shape[2]
-    block = pl.BlockSpec((1, steps, half, height), lambda g, core: (g, 0, 0, 0))
     return pl.pallas_call(
         panel_kernel,
-        grid_spec=pltpu.PrefetchScalarGridSpec(
-            num_scalar_prefetch=1,
-            grid=(groups,),
-            in_specs=[block, block, pl.BlockSpec(rows.shape, lambda g, core: (0, 0, 0))],
-            out_specs=pl.BlockSpec((1, height, width), lambda g, core: (g, 0, 0)),
-        ),
+        grid=(groups,),
+        in_specs=[
+            pl.BlockSpec((1, parts, steps, half, height), lambda g: (g, 0, 0, 0, 0)),
+            pl.BlockSpec(rows.shape, lambda g: (0, 0, 0)),
+        ],
+        out_specs=pl.BlockSpec((1, height, width), lambda g: (g, 0, 0)),
         out_shape=jax.ShapeDtypeStruct((groups, height, width), jnp.bfloat16),
         compiler_params=pltpu.CompilerParams(vmem_limit_bytes=VMEM_BYTES),
         cost_estimate=pl.CostEstimate(
@@ -71,7 +68,7 @@
             bytes_accessed=7 * 1024 * 1024,
             transcendentals=0,
         ),
-    )(core, own, other, rows)
+    )(block, rows)
 
 
 def diagonal_kernel(left_ref, right_ref, out_ref):
@@ -124,18 +121,17 @@
         swap_halves(jnp.where(first, masked[0], masked[1]), jnp.where(first, masked[1], masked[0])), axis=1
     )
     turned_block = move(inverse_block.T, TURN)
+    turned_block, wide = lax.optimization_barrier((turned_block, wide))
     turned_panel = move(wide, TURN)
     block_parts = lax.all_gather(turned_block, "zl")
-    own = lax.all_gather(block_parts, "x")
+    block = lax.all_gather(block_parts, ("x", "core")).reshape((4, 2) + block_parts.shape)
     turned_panel, block_parts = lax.optimization_barrier((turned_panel, block_parts))
     panel_parts = lax.all_gather(turned_panel, "zl")
     columns = lax.all_gather(panel_parts, "x")
     wide, panel_parts = lax.optimization_barrier((wide, panel_parts))
     rows = lax.all_gather(wide, "zh")
-    own, rows = lax.optimization_barrier((own, rows))
-    other = move(own, SWAP_CORES)
-
-    partial = panel_partial(jnp.reshape(core, (1,)).astype(jnp.int32), own, other, rows)
+    block, rows = lax.optimization_barrier((block, rows))
+    partial = panel_partial(block, rows)
     parts = lax.all_to_all(partial, "y", split_axis=0, concat_axis=0, tiled=True)
     panel = (-(jnp.sum(parts.astype(jnp.float32), axis=0) * weight)).astype(jnp.bfloat16)
     panel_rows = lax.all_gather(panel, "y")

time: 213 us -> 200 us (0.939)
  waiting for transfers between devices: 68.2 us -> 60.6 us
  starting transfers between devices: 27.1 us -> 22.5 us
  Pallas kernels: 6.23 us -> 10.4 us
  local copies, waits for them, and re-layouts: 3.71 us -> 0.16 us
  blocking collectives: 89.7 us -> 87.5 us
    ppermute x5 -> x4, waiting for transfers between devices: 26.9 us -> 19.5 us  [move(): return lax.ppermute(value, AXES, listed)]
    unnamed x8 -> x4, local copies, waits for them, and re-layouts: 3.64 us -> 0.09 us
    ppermute x5 -> x4, starting transfers between devices: 16.7 us -> 14 us  [move(): return lax.ppermute(value, AXES, listed)]
    pallas_call x1, Pallas kernels: 3.31 us -> 5.58 us  [panel_partial(): pl.pallas_call(panel_kernel, grid=(groups,), in_specs=[pl.BlockSpec((1, p...]
  transfers between devices with their start and end apart: 9 -> 8, of which waited for: 7 -> 5; matrix products, arithmetic and copies ran while one was open for 1% -> 1% of each run, Pallas kernels for 2% -> 3%
where the time goes in v3:
time: 200 us; the launch traced here: 199 us
  blocking collectives  87.5 us (44%)
  waiting for transfers between devices  60.6 us (30%)
  starting transfers between devices  22.5 us (11%)
  between operations  14.2 us (7%)
  Pallas kernels  10.4 us (5%)
  other arithmetic  3.74 us (2%)
    all_gather x1, blocking collectives, on_device(): rows = lax.all_gather(wide, 'zh')  35.9 us
    all_to_all x1, waiting for transfers between devices, on_device(): lax.all_to_all(shares, ('zh', 'core'), split_axis=0, concat_axis=0, tiled...  30.1 us
    ppermute x4, waiting for transfers between devices, move(): return lax.ppermute(value, AXES, listed)  19.5 us
    all_gather x1, blocking collectives, on_device(): panel_parts = lax.all_gather(turned_panel, 'zl')  19.4 us
    all_gather x1, blocking collectives, on_device(): block_parts = lax.all_gather(turned_block, 'zl')  18.1 us
    all_gather x1, blocking collectives, on_device(): panel_rows = lax.all_gather(panel, 'y')  14.1 us
    ppermute x4, starting transfers between devices, move(): return lax.ppermute(value, AXES, listed)  14 us
    all_to_all x1, waiting for transfers between devices, on_device(): lax.all_to_all(partial, 'y', split_axis=0, concat_axis=0, tiled=True)  11 us
  transfers between devices with their start and end apart: 8, of which 5 were waited for; matrix products, arithmetic and copies ran while one was open for 1% of the time, Pallas kernels for 3%

profile of v3, /device:TPU:6, one launch (start us, length us, event | category | flops | bytes accessed | tf_op | source)
XLA Modules:
  0.0 199.0 jit_solution(15470874732405346503)
XLA Ops:
  7.2 0.0 all-gather.8.cloned.1.call-start
  7.2 0.8 dynamic-slice_convert_fusion
  8.0 0.1 broadcast_bitcast_fusion.1
  8.1 1.1 broadcast_multiply_fusion
  9.2 1.9 collective-permute-start.1
  11.1 4.8 %collective-permute-start = (bf16[192,384]{1,0:T(8,128)(2,1)}, bf16[192,384]{1,0:T(8,128)(2,1)S(1)}, u32[]{:S(2)}, u32[]{:S(2)}) collective-permute-start(bf16[192,384]{1,0:T(8,128)(2,1)} %bitcast.44), channel_id=1, source_target_pairs={{0,0},{1,1},{2,32},{3,33},{4,64},{5,65},{6,96},{7,97},{8,8},{9,9},... | collective-permute-start | bytes 442376 | tf_op jit(solution)/shard_map/ppermute | solution.py:38
  16.0 0.0 collective-permute-done.1
  16.0 9.9 %collective-permute-done = bf16[192,384]{1,0:T(8,128)(2,1)S(1)} collective-permute-done((bf16[192,384]{1,0:T(8,128)(2,1)}, bf16[192,384]{1,0:T(8,128)(2,1)S(1)}, u32[]{:S(2)}, u32[]{:S(2)}) %collective-permute-start) | collective-permute-done | bytes 147488 | tf_op jit(solution)/shard_map/ppermute | solution.py:38
  25.9 18.1 %all-gather = bf16[768,384]{1,0:T(8,128)(2,1)} all-gather(bf16[192,384]{1,0:T(8,128)(2,1)S(1)} %collective-permute-done), channel_id=2, replica_groups=mesh['zh'=4,'y'=4,'zl'=4,'x'=4,'core'=2] {'zl'}, dimensions={0}, use_global_device_ids=true | all-gather | bytes 737280 | tf_op jit(solution)/shard_map/all_gather | solution.py:126
  44.0 0.0 all-gather.8.cloned.1.call-update
  44.0 0.0 all-gather.10.cloned.1.call-start
  44.1 4.8 %collective-permute-start.2 = (bf16[384,256]{1,0:T(8,128)(2,1)S(1)}, bf16[384,256]{1,0:T(8,128)(2,1)S(1)}, u32[]{:S(2)}, u32[]{:S(2)}) collective-permute-start(bf16[384,256]{1,0:T(8,128)(2,1)S(1)} %pad_maximum_fusion), channel_id=1, source_target_pairs={{0,0},{1,1},{2,32},{3,33},{4,64},{5,65},{6,96},{7,97},{8,8},{9,9},... | collective-permute-start | bytes 589832 | tf_op jit(solution)/shard_map/ppermute | solution.py:38
  48.9 8.6 %collective-permute-done.2 = bf16[384,256]{1,0:T(8,128)(2,1)S(1)} collective-permute-done((bf16[384,256]{1,0:T(8,128)(2,1)S(1)}, bf16[384,256]{1,0:T(8,128)(2,1)S(1)}, u32[]{:S(2)}, u32[]{:S(2)}) %collective-permute-start.2) | collective-permute-done | bytes 196640 | tf_op jit(solution)/shard_map/ppermute | solution.py:38
  57.5 19.4 %all-gather.2 = bf16[1536,256]{1,0:T(8,128)(2,1)} all-gather(bf16[384,256]{1,0:T(8,128)(2,1)S(1)} %collective-permute-done.2), channel_id=4, replica_groups=mesh['zh'=4,'y'=4,'zl'=4,'x'=4,'core'=2] {'zl'}, dimensions={0}, use_global_device_ids=true | all-gather | bytes 983040 | tf_op jit(solution)/shard_map/all_gather | solution.py:129
  76.9 0.0 all-gather.10.cloned.1.call-update
  77.0 35.9 %all-gather.3 = bf16[1536,256]{1,0:T(8,128)(2,1)} all-gather(bf16[384,256]{1,0:T(8,128)(2,1)S(1)} %pad_maximum_fusion), channel_id=5, replica_groups=mesh['zh'=4,'y'=4,'zl'=4,'x'=4,'core'=2] {'zh'}, dimensions={0}, use_global_device_ids=true | all-gather | bytes 983040 | tf_op jit(solution)/shard_map/all_gather | solution.py:132
  112.9 5.6 %shard_map.59 = bf16[4,384,256]{2,1,0:T(8,128)(2,1)} custom-call(bf16[4,2,4,192,384]{4,3,2,1,0:T(8,128)(2,1)} %bitcast.36, bf16[4,384,256]{2,1,0:T(8,128)(2,1)} %bitcast.37), custom_call_target="tpu_custom_call" | custom-call | flops 1207959552 | bytes 7340032 | tf_op jit(solution)/shard_map/pallas_call | solution.py:56
  118.5 3.5 %all-to-all-start = ((bf16[4,384,256]{2,1,0:T(8,128)(2,1)}), bf16[4,384,256]{2,1,0:T(8,128)(2,1)S(1)}, u32[]{:S(2)}, u32[]{:S(2)}) async-start(bf16[4,384,256]{2,1,0:T(8,128)(2,1)} %shard_map.59), calls=%async_computation | async-start | bytes 1572864 | tf_op jit(solution)/shard_map/all_to_all | solution.py:135
  122.0 0.1 broadcast_bitcast_fusion
  122.1 11.0 %all-to-all-done = bf16[4,384,256]{2,1,0:T(8,128)(2,1)S(1)} async-done(((bf16[4,384,256]{2,1,0:T(8,128)(2,1)}), bf16[4,384,256]{2,1,0:T(8,128)(2,1)S(1)}, u32[]{:S(2)}, u32[]{:S(2)}) %all-to-all-start) | async-done | bytes 786464 | tf_op jit(solution)/shard_map/all_to_all | solution.py:135
  133.1 0.1 convert_reduce_fusion
  133.2 0.1 fusion.1
  133.3 14.1 %all_gather.44.right_ref = bf16[4,384,256]{2,1,0:T(8,128)(2,1)} all-gather(bf16[1,384,256]{2,1,0:T(8,128)(2,1)S(1)} %fusion.1), channel_id=1, replica_groups=mesh['zh'=4,'y'=4,'zl'=4,'x'=4,'core'=2] {'y'}, dimensions={0}, use_global_device_ids=true | all-gather | bytes 983040 | tf_op jit(solution)/shard_map/all_gather | solution.py:137
  147.3 4.9 %shard_map.60 = bf16[4,2,256,128]{3,2,1,0:T(8,128)(2,1)} custom-call(bf16[4,4,384,256]{3,2,1,0:T(8,128)(2,1)} %bitcast.38, bf16[4,384,256]{2,1,0:T(8,128)(2,1)} %all_gather.44.right_ref), custom_call_target="tpu_custom_call" | custom-call | flops 805306368 | bytes 5242880 | tf_op jit(solution)/shard_map/pallas_call | solution.py:87
  152.2 4.9 %all-to-all-start.1 = ((bf16[8,256,128]{2,1,0:T(8,128)(2,1)}), bf16[8,256,128]{2,1,0:T(8,128)(2,1)S(1)}, u32[]{:S(2)}, u32[]{:S(2)}) async-start(bf16[8,256,128]{2,1,0:T(8,128)(2,1)} %bitcast.41), calls=%async_computation.1 | async-start | bytes 1048576 | tf_op jit(solution)/shard_map/all_to_all | solution.py:144
  157.1 0.1 negate_convert_fusion
  157.2 2.4 %collective-permute-start.3 = (bf16[384,128]{1,0:T(8,128)(2,1)S(1)}, bf16[384,128]{1,0:T(8,128)(2,1)S(1)}, u32[]{:S(2)}, u32[]{:S(2)}) collective-permute-start(bf16[384,128]{1,0:T(8,128)(2,1)S(1)} %broadcast_select_fusion.1), channel_id=1, source_target_pairs={{0,1},{1,0},{2,3},{3,2},{4,5},{5,4},{6,7},{7,6},{8,9},{9,8},{10,11... | collective-permute-start | bytes 294920 | tf_op jit(solution)/shard_map/ppermute | solution.py:38
  159.7 0.9 collective-permute-done.3
  160.6 0.7 pad_maximum_fusion.1
  161.3 30.1 %all-to-all-done.1 = bf16[8,256,128]{2,1,0:T(8,128)(2,1)S(1)} async-done(((bf16[8,256,128]{2,1,0:T(8,128)(2,1)}), bf16[8,256,128]{2,1,0:T(8,128)(2,1)S(1)}, u32[]{:S(2)}, u32[]{:S(2)}) %all-to-all-start.1) | async-done | bytes 524320 | tf_op jit(solution)/shard_map/all_to_all | solution.py:144
  191.4 0.1 convert_reduce_fusion.1
  191.5 0.7 subtract_convert_fusion
  (11 shorter events, 0.1 us)
Async XLA Ops:
  7.2 105.8 %all-gather.8.cloned.1.call-start = ((), (), s32[]{:S(2)}) async-start(), calls=%async_computation.2 | async-start | bytes 5308416 | tf_op jit(solution)/shard_map/all_gather | solution.py:127
  9.2 6.8 %collective-permute-start.1 = (bf16[384,128]{1,0:T(8,128)(2,1)S(1)}, bf16[384,128]{1,0:T(8,128)(2,1)S(1)}, u32[]{:S(2)}, u32[]{:S(2)}) collective-permute-start(bf16[384,128]{1,0:T(8,128)(2,1)S(1)} %select_bitcast_fusion.2), channel_id=1, source_target_pairs={{0,1},{1,0},{2,3},{3,2},{4,5},{5,4},{6,7},{7,6},{8,9},{9,8},{10,11... | collective-permute-start | bytes 294920 | tf_op jit(solution)/shard_map/ppermute | solution.py:38
  11.1 14.8 %collective-permute-start = (bf16[192,384]{1,0:T(8,128)(2,1)}, bf16[192,384]{1,0:T(8,128)(2,1)S(1)}, u32[]{:S(2)}, u32[]{:S(2)}) collective-permute-start(bf16[192,384]{1,0:T(8,128)(2,1)} %bitcast.44), channel_id=1, source_target_pairs={{0,0},{1,1},{2,32},{3,33},{4,64},{5,65},{6,96},{7,97},{8,8},{9,9},... | collective-permute-start | bytes 442376 | tf_op jit(solution)/shard_map/ppermute | solution.py:38
  44.0 103.3 %all-gather.10.cloned.1.call-start = ((), (), s32[]{:S(2)}) async-start(), calls=%async_computation.3 | async-start | bytes 3932160 | tf_op jit(solution)/shard_map/all_gather | solution.py:130
  44.1 13.5 %collective-permute-start.2 = (bf16[384,256]{1,0:T(8,128)(2,1)S(1)}, bf16[384,256]{1,0:T(8,128)(2,1)S(1)}, u32[]{:S(2)}, u32[]{:S(2)}) collective-permute-start(bf16[384,256]{1,0:T(8,128)(2,1)S(1)} %pad_maximum_fusion), channel_id=1, source_target_pairs={{0,0},{1,1},{2,32},{3,33},{4,64},{5,65},{6,96},{7,97},{8,8},{9,9},... | collective-permute-start | bytes 589832 | tf_op jit(solution)/shard_map/ppermute | solution.py:38
  118.5 14.6 %all-to-all-start = ((bf16[4,384,256]{2,1,0:T(8,128)(2,1)}), bf16[4,384,256]{2,1,0:T(8,128)(2,1)S(1)}, u32[]{:S(2)}, u32[]{:S(2)}) async-start(bf16[4,384,256]{2,1,0:T(8,128)(2,1)} %shard_map.59), calls=%async_computation | async-start | bytes 1572864 | tf_op jit(solution)/shard_map/all_to_all | solution.py:135
  147.3 44.1 %copy-start = (bf16[2,256,128]{2,1,0:T(8,128)(2,1)S(1)}, bf16[2,256,128]{2,1,0:T(8,128)(2,1)}, u32[]{:S(2)}) copy-start(bf16[2,256,128]{2,1,0:T(8,128)(2,1)} %param.7) | copy-start | bytes 393220
  152.2 39.2 %all-to-all-start.1 = ((bf16[8,256,128]{2,1,0:T(8,128)(2,1)}), bf16[8,256,128]{2,1,0:T(8,128)(2,1)S(1)}, u32[]{:S(2)}, u32[]{:S(2)}) async-start(bf16[8,256,128]{2,1,0:T(8,128)(2,1)} %bitcast.41), calls=%async_computation.1 | async-start | bytes 1048576 | tf_op jit(solution)/shard_map/all_to_all | solution.py:144
  157.2 3.3 %collective-permute-start.3 = (bf16[384,128]{1,0:T(8,128)(2,1)S(1)}, bf16[384,128]{1,0:T(8,128)(2,1)S(1)}, u32[]{:S(2)}, u32[]{:S(2)}) collective-permute-start(bf16[384,128]{1,0:T(8,128)(2,1)S(1)} %broadcast_select_fusion.1), channel_id=1, source_target_pairs={{0,1},{1,0},{2,3},{3,2},{4,5},{5,4},{6,7},{7,6},{8,9},{9,8},{10,11... | collective-permute-start | bytes 294920 | tf_op jit(solution)/shard_map/ppermute | solution.py:38
Sparse Core Ops, SparseCore 0:
  44.1 40.6 all-gather.7
  86.9 47.2 all-gather.9

commit v4 on v3

--- a/solution.py
+++ b/solution.py
@@ -32,6 +32,7 @@
 
 SWAP_CORES = pairs(lambda zh, y, zl, x, core: (zh, y, zl, x, 1 - core))
 TURN = pairs(lambda zh, y, zl, x, core: (zh, x, zl, y, core))
+TURN_AND_SWAP = pairs(lambda zh, y, zl, x, core: (zh, x, zl, y, 1 - core))
 
 
 def move(value, listed):
@@ -77,9 +78,7 @@
         total += lax.dot_general(
             left_ref[y, 0], right_ref[y], CONTRACT_ROWS, preferred_element_type=jnp.float32
         )
-    value = total.astype(out_ref.dtype)
-    out_ref[0, 0] = value[:, :128]
-    out_ref[0, 1] = value[:, 128:]
+    out_ref[0] = total.astype(out_ref.dtype)
 
 
 def diagonal_partial(left, right):
@@ -91,8 +90,8 @@
             pl.BlockSpec((groups, 1, depth, width), lambda g: (0, g, 0, 0)),
             pl.BlockSpec(right.shape, lambda g: (0, 0, 0)),
         ],
-        out_specs=pl.BlockSpec((1, 2, width, 128), lambda g: (g, 0, 0, 0)),
-        out_shape=jax.ShapeDtypeStruct((4, 2, width, 128), jnp.bfloat16),
+        out_specs=pl.BlockSpec((1, width, 256), lambda g: (g, 0, 0)),
+        out_shape=jax.ShapeDtypeStruct((4, width, 256), jnp.bfloat16),
         compiler_params=pltpu.CompilerParams(vmem_limit_bytes=VMEM_BYTES),
         cost_estimate=pl.CostEstimate(
             flops=2 * groups * steps * depth * width * 256,
@@ -102,48 +101,61 @@
     )(left, right)
 
 
+def mask_kernel(value_ref, flag_ref, out_ref):
+    out_ref[...] = value_ref[...] * flag_ref[...]
+
+
+def masked_rows(value, flag):
+    return pl.pallas_call(
+        mask_kernel,
+        out_shape=jax.ShapeDtypeStruct(value.shape, value.dtype),
+        compiler_params=pltpu.CompilerParams(vmem_limit_bytes=VMEM_BYTES),
+        cost_estimate=pl.CostEstimate(flops=400 * 10**9, bytes_accessed=10**6, transcendentals=0),
+    )(value, flag)
+
+
 def on_device(inverse_block, panels, structure, pivot_inverse):
+    zh, y, x = (lax.axis_index(name) for name in ("zh", "y", "x"))
     core = lax.axis_index("core")
     first = core == 0
-    row_index = lax.axis_index("zh") * 4 + lax.axis_index("y")
     local_rows = panels.shape[1]
     tiles_here = local_rows // TILE
-    tile_flags = lax.dynamic_slice_in_dim(structure, row_index * tiles_here, tiles_here, 1)
-    row_flags = jnp.repeat(tile_flags, TILE, axis=1).astype(jnp.bfloat16)
-    masked = panels * row_flags[:, :, None]
-    weight = jnp.where(first, row_flags[0], row_flags[1]).astype(jnp.float32)[:, None]
 
-    def swap_halves(mine, theirs):
-        got = move(theirs, SWAP_CORES)
-        return jnp.where(first, mine, got), jnp.where(first, got, mine)
+    def flags(group):
+        start = (zh * 4 + group) * tiles_here
+        here = lax.dynamic_slice(structure, (core, start), (1, tiles_here))
+        return jnp.repeat(here[0], TILE)[:, None]
 
-    wide = jnp.concatenate(
-        swap_halves(jnp.where(first, masked[0], masked[1]), jnp.where(first, masked[1], masked[0])), axis=1
-    )
-    turned_block = move(inverse_block.T, TURN)
-    turned_block, wide = lax.optimization_barrier((turned_block, wide))
-    turned_panel = move(wide, TURN)
-    block_parts = lax.all_gather(turned_block, "zl")
-    block = lax.all_gather(block_parts, ("x", "core")).reshape((4, 2) + block_parts.shape)
-    turned_panel, block_parts = lax.optimization_barrier((turned_panel, block_parts))
-    panel_parts = lax.all_gather(turned_panel, "zl")
-    columns = lax.all_gather(panel_parts, "x")
-    wide, panel_parts = lax.optimization_barrier((wide, panel_parts))
-    rows = lax.all_gather(wide, "zh")
-    block, rows = lax.optimization_barrier((block, rows))
+    def own_and_other(pair):
+        return jnp.where(first, pair[0], pair[1]), jnp.where(first, pair[1], pair[0])
+
+    mine, theirs = own_and_other(panels)
+    wide = jnp.concatenate(own_and_other((mine, move(theirs, SWAP_CORES))), axis=1)
+    turned = move(wide, TURN)
+    wide = wide * flags(y).astype(jnp.bfloat16)
+
+    block_parts = lax.all_gather(inverse_block.T, "zl")
+    block = lax.all_gather(block_parts, ("y", "core")).reshape((4, 2) + block_parts.shape)
+    wide, block_parts = lax.optimization_barrier((wide, block_parts))
+    panel_parts = lax.all_gather(wide, "zl")
+    turned, panel_parts = lax.optimization_barrier((turned, panel_parts))
+    rows = lax.all_gather(masked_rows(turned, flags(x).astype(jnp.bfloat16)), "zh")
+    columns = lax.all_gather(panel_parts, "y")
+
     partial = panel_partial(block, rows)
-    parts = lax.all_to_all(partial, "y", split_axis=0, concat_axis=0, tiled=True)
+    parts = lax.all_to_all(partial, "x", split_axis=0, concat_axis=0, tiled=True)
+    weight = flags(x).astype(jnp.float32)
     panel = (-(jnp.sum(parts.astype(jnp.float32), axis=0) * weight)).astype(jnp.bfloat16)
-    panel_rows = lax.all_gather(panel, "y")
-    left, right = panel[:, :128], panel[:, 128:]
-    panel_inverse = jnp.stack(
-        swap_halves(jnp.where(first, left, right), jnp.where(first, right, left))
-    )
+    panel_rows = lax.all_gather(panel, "x")
+    mine, theirs = own_and_other((panel[:, :128], panel[:, 128:]))
+    panel_inverse = jnp.stack(own_and_other((move(mine, TURN), move(theirs, TURN_AND_SWAP))))
 
-    shares = diagonal_partial(columns, panel_rows).reshape(8, 256, 128)
-    shares = lax.all_to_all(shares, ("zh", "core"), split_axis=0, concat_axis=0, tiled=True)
-    summed = jnp.sum(shares.reshape(4, 2, 256, 128).astype(jnp.float32), axis=0)
-    diagonal_inverse = (pivot_inverse.astype(jnp.float32) - summed).astype(jnp.bfloat16)
+    shares = diagonal_partial(columns, panel_rows)
+    shares = lax.all_to_all(shares, "zh", split_axis=0, concat_axis=0, tiled=True)
+    summed = jnp.sum(shares.astype(jnp.float32), axis=0).astype(jnp.bfloat16)
+    mine, theirs = own_and_other((summed[:, :128], summed[:, 128:]))
+    summed = jnp.stack(own_and_other((move(mine, TURN), move(theirs, TURN_AND_SWAP))))
+    diagonal_inverse = (pivot_inverse.astype(jnp.float32) - summed.astype(jnp.float32)).astype(jnp.bfloat16)
     return (panel_inverse, diagonal_inverse)
 
 

time: 200 us -> 190 us (0.950)
  the two profiles are of different devices: /device:TPU:6 before, /device:TPU:14 now
where the time goes in v4:
time: 190 us; the launch traced here: 189 us
  blocking collectives  89.6 us (47%)
  starting transfers between devices  35.1 us (18%)
  waiting for transfers between devices  31.1 us (16%)
  between operations  14.2 us (7%)
  Pallas kernels  12.2 us (6%)
  other arithmetic  5.26 us (3%)
    all_gather x1, blocking collectives, on_device(): lax.all_gather(masked_rows(turned, flags(x).astype(jnp.bfloat16)), 'zh')  36 us
    ppermute x6, starting transfers between devices, move(): return lax.ppermute(value, AXES, listed)  23.7 us
    all_gather x1, blocking collectives, on_device(): block_parts = lax.all_gather(inverse_block.T, 'zl')  19.9 us
    all_gather x1, blocking collectives, on_device(): panel_parts = lax.all_gather(wide, 'zl')  18.7 us
    all_gather x1, blocking collectives, on_device(): panel_rows = lax.all_gather(panel, 'x')  15.1 us
    ppermute x6, waiting for transfers between devices, move(): return lax.ppermute(value, AXES, listed)  15 us
    all_to_all x1, waiting for transfers between devices, on_device(): lax.all_to_all(shares, 'zh', split_axis=0, concat_axis=0, tiled=True)  8.6 us
    all_to_all x1, waiting for transfers between devices, on_device(): lax.all_to_all(partial, 'x', split_axis=0, concat_axis=0, tiled=True)  7.5 us
  transfers between devices with their start and end apart: 10, of which 5 were waited for; matrix products, arithmetic and copies ran while one was open for 3% of the time, Pallas kernels for 4%

profile of v4, /device:TPU:14, one launch (start us, length us, event | category | flops | bytes accessed | tf_op | source)
XLA Modules:
  0.0 189.2 jit_solution(6745196972880388389)
XLA Ops:
  7.2 19.9 %all-gather = bf16[768,384]{1,0:T(8,128)(2,1)} all-gather(bf16[192,384]{1,0:T(8,128)(2,1)} %bitcast.47), channel_id=2, replica_groups=mesh['zh'=4,'y'=4,'zl'=4,'x'=4,'core'=2] {'zl'}, dimensions={0}, use_global_device_ids=true | all-gather | bytes 737280 | tf_op jit(solution)/shard_map/all_gather | solution.py:137
  27.2 1.0 select_bitcast_fusion.2
  28.1 1.9 %collective-permute-start = (bf16[384,128]{1,0:T(8,128)(2,1)S(1)}, bf16[384,128]{1,0:T(8,128)(2,1)S(1)}, u32[]{:S(2)}, u32[]{:S(2)}) collective-permute-start(bf16[384,128]{1,0:T(8,128)(2,1)S(1)} %select_bitcast_fusion.2), channel_id=1, source_target_pairs={{0,1},{1,0},{2,3},{3,2},{4,5},{5,4},{6,7},{7,6},{8,9},{9,8},{10,11... | collective-permute-start | bytes 294920 | tf_op jit(solution)/shard_map/ppermute | solution.py:39
  30.1 1.3 convert_bitcast_fusion
  31.6 0.8 copy.9
  32.4 1.0 bitcast_select_fusion.1
  33.3 0.1 broadcast_multiply_fusion
  33.4 5.0 %collective-permute-start.1 = (bf16[384,256]{1,0:T(8,128)(2,1)S(1)}, bf16[384,256]{1,0:T(8,128)(2,1)S(1)}, u32[]{:S(2)}, u32[]{:S(2)}) collective-permute-start(bf16[384,256]{1,0:T(8,128)(2,1)S(1)} %get-tuple-element.15), channel_id=1, source_target_pairs={{0,0},{1,1},{2,32},{3,33},{4,64},{5,65},{6,96},{7,97},{8,8},{9,9},... | collective-permute-start | bytes 589832 | tf_op jit(solution)/shard_map/ppermute | solution.py:39
  38.5 18.7 %all-gather.2 = bf16[1536,256]{1,0:T(8,128)(2,1)} all-gather(bf16[384,256]{1,0:T(8,128)(2,1)S(1)} %get-tuple-element.5), channel_id=4, replica_groups=mesh['zh'=4,'y'=4,'zl'=4,'x'=4,'core'=2] {'zl'}, dimensions={0}, use_global_device_ids=true | all-gather | bytes 983040 | tf_op jit(solution)/shard_map/all_gather | solution.py:140
  57.2 0.7 copy-done.2
  57.9 1.8 shard_map.59
  59.7 36.0 %all-gather.3 = bf16[1536,256]{1,0:T(8,128)(2,1)} all-gather(bf16[384,256]{1,0:T(8,128)(2,1)} %shard_map.59), channel_id=5, replica_groups=mesh['zh'=4,'y'=4,'zl'=4,'x'=4,'core'=2] {'zh'}, dimensions={0}, use_global_device_ids=true | all-gather | bytes 983040 | tf_op jit(solution)/shard_map/all_gather | solution.py:142
  95.6 5.6 %shard_map.60 = bf16[4,384,256]{2,1,0:T(8,128)(2,1)} custom-call(bf16[4,2,4,192,384]{4,3,2,1,0:T(8,128)(2,1)} %bitcast.42, bf16[4,384,256]{2,1,0:T(8,128)(2,1)} %bitcast.43), custom_call_target="tpu_custom_call" | custom-call | flops 1207959552 | bytes 7340032 | tf_op jit(solution)/shard_map/pallas_call | solution.py:57
  101.2 4.5 %all-to-all-start = ((bf16[4,384,256]{2,1,0:T(8,128)(2,1)}), bf16[4,384,256]{2,1,0:T(8,128)(2,1)S(1)}, u32[]{:S(2)}, u32[]{:S(2)}) async-start(bf16[4,384,256]{2,1,0:T(8,128)(2,1)} %shard_map.60), calls=%async_computation | async-start | bytes 1572864 | tf_op jit(solution)/shard_map/all_to_all | solution.py:146
  105.8 7.5 %all-to-all-done = bf16[4,384,256]{2,1,0:T(8,128)(2,1)S(1)} async-done(((bf16[4,384,256]{2,1,0:T(8,128)(2,1)}), bf16[4,384,256]{2,1,0:T(8,128)(2,1)S(1)}, u32[]{:S(2)}, u32[]{:S(2)}) %all-to-all-start) | async-done | bytes 786464 | tf_op jit(solution)/shard_map/all_to_all | solution.py:146
  113.3 0.1 convert_reduce_fusion
  113.4 0.1 fusion.1
  113.5 15.1 %all_gather.44.right_ref = bf16[4,384,256]{2,1,0:T(8,128)(2,1)} all-gather(bf16[1,384,256]{2,1,0:T(8,128)(2,1)S(1)} %fusion.1), channel_id=1, replica_groups=mesh['zh'=4,'y'=4,'zl'=4,'x'=4,'core'=2] {'x'}, dimensions={0}, use_global_device_ids=true | all-gather | bytes 983040 | tf_op jit(solution)/shard_map/all_gather | solution.py:149
  128.6 4.9 %shard_map.61 = bf16[4,256,256]{2,1,0:T(8,128)(2,1)} custom-call(bf16[4,4,384,256]{3,2,1,0:T(8,128)(2,1)} %bitcast.44, bf16[4,384,256]{2,1,0:T(8,128)(2,1)} %all_gather.44.right_ref), custom_call_target="tpu_custom_call" | custom-call | flops 805306368 | bytes 5242880 | tf_op jit(solution)/shard_map/pallas_call | solution.py:86
  133.5 6.8 %all-to-all-start.1 = ((bf16[4,256,256]{2,1,0:T(8,128)(2,1)}), bf16[4,256,256]{2,1,0:T(8,128)(2,1)S(1)}, u32[]{:S(2)}, u32[]{:S(2)}) async-start(bf16[4,256,256]{2,1,0:T(8,128)(2,1)} %shard_map.61), calls=%async_computation.1 | async-start | bytes 1048576 | tf_op jit(solution)/shard_map/all_to_all | solution.py:154
  140.3 0.1 negate_convert_fusion
  140.4 4.6 %collective-permute-start.2 = (bf16[384,128]{1,0:T(8,128)(2,1)S(1)}, bf16[384,128]{1,0:T(8,128)(2,1)S(1)}, u32[]{:S(2)}, u32[]{:S(2)}) collective-permute-start(bf16[384,128]{1,0:T(8,128)(2,1)S(1)} %get-tuple-element.12), channel_id=1, source_target_pairs={{0,0},{1,1},{2,32},{3,33},{4,64},{5,65},{6,96},{7,97},{8,8},{9,9},... | collective-permute-start | bytes 294920 | tf_op jit(solution)/shard_map/ppermute | solution.py:39
  145.0 1.9 %collective-permute-start.3 = (bf16[384,128]{1,0:T(8,128)(2,1)S(1)}, bf16[384,128]{1,0:T(8,128)(2,1)S(1)}, u32[]{:S(2)}, u32[]{:S(2)}) collective-permute-start(bf16[384,128]{1,0:T(8,128)(2,1)S(1)} %get-tuple-element.13), channel_id=1, source_target_pairs={{0,1},{1,0},{2,33},{3,32},{4,65},{5,64},{6,97},{7,96},{8,9},{9,8},... | collective-permute-start | bytes 294920 | tf_op jit(solution)/shard_map/ppermute | solution.py:39
  146.9 5.0 %collective-permute-done.2 = bf16[384,128]{1,0:T(8,128)(2,1)S(1)} collective-permute-done((bf16[384,128]{1,0:T(8,128)(2,1)S(1)}, bf16[384,128]{1,0:T(8,128)(2,1)S(1)}, u32[]{:S(2)}, u32[]{:S(2)}) %collective-permute-start.2) | collective-permute-done | bytes 98336 | tf_op jit(solution)/shard_map/ppermute | solution.py:39
  151.9 3.2 %collective-permute-done.3 = bf16[384,128]{1,0:T(8,128)(2,1)S(1)} collective-permute-done((bf16[384,128]{1,0:T(8,128)(2,1)S(1)}, bf16[384,128]{1,0:T(8,128)(2,1)S(1)}, u32[]{:S(2)}, u32[]{:S(2)}) %collective-permute-start.3) | collective-permute-done | bytes 98336 | tf_op jit(solution)/shard_map/ppermute | solution.py:39
  155.1 8.6 %all-to-all-done.1 = bf16[4,256,256]{2,1,0:T(8,128)(2,1)S(1)} async-done(((bf16[4,256,256]{2,1,0:T(8,128)(2,1)}), bf16[4,256,256]{2,1,0:T(8,128)(2,1)S(1)}, u32[]{:S(2)}, u32[]{:S(2)}) %all-to-all-start.1) | async-done | bytes 524320 | tf_op jit(solution)/shard_map/all_to_all | solution.py:154
  163.7 0.1 reduce_sum.25
  163.8 8.3 %collective-permute-start.4 = (bf16[256,128]{1,0:T(8,128)(2,1)S(1)}, bf16[256,128]{1,0:T(8,128)(2,1)S(1)}, u32[]{:S(2)}, u32[]{:S(2)}) collective-permute-start(bf16[256,128]{1,0:T(8,128)(2,1)S(1)} %get-tuple-element.18), channel_id=1, source_target_pairs={{0,0},{1,1},{2,32},{3,33},{4,64},{5,65},{6,96},{7,97},{8,8},{9,9},... | collective-permute-start | bytes 196616 | tf_op jit(solution)/shard_map/ppermute | solution.py:39
  172.1 1.9 %collective-permute-start.5 = (bf16[256,128]{1,0:T(8,128)(2,1)S(1)}, bf16[256,128]{1,0:T(8,128)(2,1)S(1)}, u32[]{:S(2)}, u32[]{:S(2)}) collective-permute-start(bf16[256,128]{1,0:T(8,128)(2,1)S(1)} %get-tuple-element.19), channel_id=1, source_target_pairs={{0,1},{1,0},{2,33},{3,32},{4,65},{5,64},{6,97},{7,96},{8,9},{9,8},... | collective-permute-start | bytes 196616 | tf_op jit(solution)/shard_map/ppermute | solution.py:39
  174.0 0.7 pad_maximum_fusion.1
  174.7 6.9 %collective-permute-done.5 = bf16[256,128]{1,0:T(8,128)(2,1)S(1)} collective-permute-done((bf16[256,128]{1,0:T(8,128)(2,1)S(1)}, bf16[256,128]{1,0:T(8,128)(2,1)S(1)}, u32[]{:S(2)}, u32[]{:S(2)}) %collective-permute-start.5) | collective-permute-done | bytes 65568 | tf_op jit(solution)/shard_map/ppermute | solution.py:39
  181.6 0.7 subtract_convert_fusion
  (22 shorter events, 0.4 us)
Async XLA Ops:
  7.2 88.5 %all-gather.8.cloned.1.call-start = ((), (), s32[]{:S(2)}) async-start(), calls=%async_computation.2 | async-start | bytes 5308416 | tf_op jit(solution)/shard_map/all_gather | solution.py:138
  27.1 101.5 %all-gather.10.cloned.1.call-start = ((), (), s32[]{:S(2)}) async-start(), calls=%async_computation.3 | async-start | bytes 3932160 | tf_op jit(solution)/shard_map/all_gather | solution.py:143
  28.1 4.2 %collective-permute-start = (bf16[384,128]{1,0:T(8,128)(2,1)S(1)}, bf16[384,128]{1,0:T(8,128)(2,1)S(1)}, u32[]{:S(2)}, u32[]{:S(2)}) collective-permute-start(bf16[384,128]{1,0:T(8,128)(2,1)S(1)} %select_bitcast_fusion.2), channel_id=1, source_target_pairs={{0,1},{1,0},{2,3},{3,2},{4,5},{5,4},{6,7},{7,6},{8,9},{9,8},{10,11... | collective-permute-start | bytes 294920 | tf_op jit(solution)/shard_map/ppermute | solution.py:39
  33.4 23.7 %collective-permute-start.1 = (bf16[384,256]{1,0:T(8,128)(2,1)S(1)}, bf16[384,256]{1,0:T(8,128)(2,1)S(1)}, u32[]{:S(2)}, u32[]{:S(2)}) collective-permute-start(bf16[384,256]{1,0:T(8,128)(2,1)S(1)} %get-tuple-element.15), channel_id=1, source_target_pairs={{0,0},{1,1},{2,32},{3,33},{4,64},{5,65},{6,96},{7,97},{8,8},{9,9},... | collective-permute-start | bytes 589832 | tf_op jit(solution)/shard_map/ppermute | solution.py:39
  57.2 0.7 copy-start.2
  95.6 10.1 %copy-start.1 = (f32[3]{0:T(128)S(1)}, f32[3]{0:T(128)}, u32[]{:S(2)}) copy-start(f32[3]{0:T(128)} %get-tuple-element.20) | copy-start | bytes 40
  101.2 12.1 %all-to-all-start = ((bf16[4,384,256]{2,1,0:T(8,128)(2,1)}), bf16[4,384,256]{2,1,0:T(8,128)(2,1)S(1)}, u32[]{:S(2)}, u32[]{:S(2)}) async-start(bf16[4,384,256]{2,1,0:T(8,128)(2,1)} %shard_map.60), calls=%async_computation | async-start | bytes 1572864 | tf_op jit(solution)/shard_map/all_to_all | solution.py:146
  128.6 53.0 %copy-start = (bf16[2,256,128]{2,1,0:T(8,128)(2,1)S(1)}, bf16[2,256,128]{2,1,0:T(8,128)(2,1)}, u32[]{:S(2)}) copy-start(bf16[2,256,128]{2,1,0:T(8,128)(2,1)} %param.7) | copy-start | bytes 393220
  133.5 30.2 %all-to-all-start.1 = ((bf16[4,256,256]{2,1,0:T(8,128)(2,1)}), bf16[4,256,256]{2,1,0:T(8,128)(2,1)S(1)}, u32[]{:S(2)}, u32[]{:S(2)}) async-start(bf16[4,256,256]{2,1,0:T(8,128)(2,1)} %shard_map.61), calls=%async_computation.1 | async-start | bytes 1048576 | tf_op jit(solution)/shard_map/all_to_all | solution.py:154
  140.4 11.4 %collective-permute-start.2 = (bf16[384,128]{1,0:T(8,128)(2,1)S(1)}, bf16[384,128]{1,0:T(8,128)(2,1)S(1)}, u32[]{:S(2)}, u32[]{:S(2)}) collective-permute-start(bf16[384,128]{1,0:T(8,128)(2,1)S(1)} %get-tuple-element.12), channel_id=1, source_target_pairs={{0,0},{1,1},{2,32},{3,33},{4,64},{5,65},{6,96},{7,97},{8,8},{9,9},... | collective-permute-start | bytes 294920 | tf_op jit(solution)/shard_map/ppermute | solution.py:39
  145.0 10.1 %collective-permute-start.3 = (bf16[384,128]{1,0:T(8,128)(2,1)S(1)}, bf16[384,128]{1,0:T(8,128)(2,1)S(1)}, u32[]{:S(2)}, u32[]{:S(2)}) collective-permute-start(bf16[384,128]{1,0:T(8,128)(2,1)S(1)} %get-tuple-element.13), channel_id=1, source_target_pairs={{0,1},{1,0},{2,33},{3,32},{4,65},{5,64},{6,97},{7,96},{8,9},{9,8},... | collective-permute-start | bytes 294920 | tf_op jit(solution)/shard_map/ppermute | solution.py:39
  163.8 11.0 %collective-permute-start.4 = (bf16[256,128]{1,0:T(8,128)(2,1)S(1)}, bf16[256,128]{1,0:T(8,128)(2,1)S(1)}, u32[]{:S(2)}, u32[]{:S(2)}) collective-permute-start(bf16[256,128]{1,0:T(8,128)(2,1)S(1)} %get-tuple-element.18), channel_id=1, source_target_pairs={{0,0},{1,1},{2,32},{3,33},{4,64},{5,65},{6,96},{7,97},{8,8},{9,9},... | collective-permute-start | bytes 196616 | tf_op jit(solution)/shard_map/ppermute | solution.py:39
  172.1 9.5 %collective-permute-start.5 = (bf16[256,128]{1,0:T(8,128)(2,1)S(1)}, bf16[256,128]{1,0:T(8,128)(2,1)S(1)}, u32[]{:S(2)}, u32[]{:S(2)}) collective-permute-start(bf16[256,128]{1,0:T(8,128)(2,1)S(1)} %get-tuple-element.19), channel_id=1, source_target_pairs={{0,1},{1,0},{2,33},{3,32},{4,65},{5,64},{6,97},{7,96},{8,9},{9,8},... | collective-permute-start | bytes 196616 | tf_op jit(solution)/shard_map/ppermute | solution.py:39
Sparse Core Ops, SparseCore 0:
  27.2 42.4 all-gather.7
  71.8 47.4 all-gather.9

commit v5 on v4

--- a/solution.py
+++ b/solution.py
@@ -30,9 +30,10 @@
     return listed
 
 
-SWAP_CORES = pairs(lambda zh, y, zl, x, core: (zh, y, zl, x, 1 - core))
+PAIR = pairs(lambda zh, y, zl, x, core: (zh, y, zl ^ 1, x, core))
+CROSS = pairs(lambda zh, y, zl, x, core: (zh, y, zl ^ 2, x, core))
 TURN = pairs(lambda zh, y, zl, x, core: (zh, x, zl, y, core))
-TURN_AND_SWAP = pairs(lambda zh, y, zl, x, core: (zh, x, zl, y, 1 - core))
+TURN_AND_PAIR = pairs(lambda zh, y, zl, x, core: (zh, x, zl ^ 1, y, core))
 
 
 def move(value, listed):
@@ -73,28 +74,30 @@
 
 
 def diagonal_kernel(left_ref, right_ref, out_ref):
-    total = jnp.zeros((left_ref.shape[3], right_ref.shape[2]), jnp.float32)
-    for y in range(4):
+    total = jnp.zeros((256, 256), jnp.float32)
+    for group in range(4):
         total += lax.dot_general(
-            left_ref[y, 0], right_ref[y], CONTRACT_ROWS, preferred_element_type=jnp.float32
+            left_ref[group, 0, 0], right_ref[group], CONTRACT_ROWS, preferred_element_type=jnp.float32
         )
-    out_ref[0] = total.astype(out_ref.dtype)
+    value = total.astype(out_ref.dtype)
+    out_ref[0, 0] = value[:128]
+    out_ref[1, 0] = value[128:]
 
 
 def diagonal_partial(left, right):
-    groups, steps, depth, width = left.shape
+    groups, cores, couples, depth, width = left.shape
     return pl.pallas_call(
         diagonal_kernel,
-        grid=(steps,),
+        grid=(couples, cores),
         in_specs=[
-            pl.BlockSpec((groups, 1, depth, width), lambda g: (0, g, 0, 0)),
-            pl.BlockSpec(right.shape, lambda g: (0, 0, 0)),
+            pl.BlockSpec((groups, 1, 1, depth, width), lambda p, c: (0, c, p, 0, 0)),
+            pl.BlockSpec(right.shape, lambda p, c: (0, 0, 0)),
         ],
-        out_specs=pl.BlockSpec((1, width, 256), lambda g: (g, 0, 0)),
-        out_shape=jax.ShapeDtypeStruct((4, width, 256), jnp.bfloat16),
+        out_specs=pl.BlockSpec((2, 1, 128, 256), lambda p, c: (p, c, 0, 0)),
+        out_shape=jax.ShapeDtypeStruct((4, cores, 128, 256), jnp.bfloat16),
         compiler_params=pltpu.CompilerParams(vmem_limit_bytes=VMEM_BYTES),
         cost_estimate=pl.CostEstimate(
-            flops=2 * groups * steps * depth * width * 256,
+            flops=2 * groups * cores * couples * depth * width * 256,
             bytes_accessed=5 * 1024 * 1024,
             transcendentals=0,
         ),
@@ -115,46 +118,44 @@
 
 
 def on_device(inverse_block, panels, structure, pivot_inverse):
-    zh, y, x = (lax.axis_index(name) for name in ("zh", "y", "x"))
-    core = lax.axis_index("core")
-    first = core == 0
+    zh, y, zl, x = (lax.axis_index(name) for name in ("zh", "y", "zl", "x"))
+    sup = lax.rem(zl, 2)
     local_rows = panels.shape[1]
     tiles_here = local_rows // TILE
 
     def flags(group):
         start = (zh * 4 + group) * tiles_here
-        here = lax.dynamic_slice(structure, (core, start), (1, tiles_here))
+        here = lax.dynamic_slice(structure, (sup, start), (1, tiles_here))
         return jnp.repeat(here[0], TILE)[:, None]
 
-    def own_and_other(pair):
-        return jnp.where(first, pair[0], pair[1]), jnp.where(first, pair[1], pair[0])
+    def ordered(position, mine, theirs):
+        first = position == 0
+        return jnp.where(first, mine, theirs), jnp.where(first, theirs, mine)
 
-    mine, theirs = own_and_other(panels)
-    wide = jnp.concatenate(own_and_other((mine, move(theirs, SWAP_CORES))), axis=1)
+    mine, theirs = ordered(sup, panels[0], panels[1])
+    wide = jnp.concatenate(ordered(sup, mine, move(theirs, PAIR)), axis=1)
     turned = move(wide, TURN)
     wide = wide * flags(y).astype(jnp.bfloat16)
 
     block_parts = lax.all_gather(inverse_block.T, "zl")
     block = lax.all_gather(block_parts, ("y", "core")).reshape((4, 2) + block_parts.shape)
-    wide, block_parts = lax.optimization_barrier((wide, block_parts))
-    panel_parts = lax.all_gather(wide, "zl")
-    turned, panel_parts = lax.optimization_barrier((turned, panel_parts))
+    panel_parts = jnp.stack(ordered(zl // 2, wide, move(wide, CROSS)))
+    columns = lax.all_gather(panel_parts, ("y", "core")).reshape((4, 2) + panel_parts.shape)
     rows = lax.all_gather(masked_rows(turned, flags(x).astype(jnp.bfloat16)), "zh")
-    columns = lax.all_gather(panel_parts, "y")
 
     partial = panel_partial(block, rows)
     parts = lax.all_to_all(partial, "x", split_axis=0, concat_axis=0, tiled=True)
     weight = flags(x).astype(jnp.float32)
     panel = (-(jnp.sum(parts.astype(jnp.float32), axis=0) * weight)).astype(jnp.bfloat16)
     panel_rows = lax.all_gather(panel, "x")
-    mine, theirs = own_and_other((panel[:, :128], panel[:, 128:]))
-    panel_inverse = jnp.stack(own_and_other((move(mine, TURN), move(theirs, TURN_AND_SWAP))))
+    mine, theirs = ordered(sup, panel[:, :128], panel[:, 128:])
+    panel_inverse = jnp.stack(ordered(sup, move(mine, TURN), move(theirs, TURN_AND_PAIR)))
 
-    shares = diagonal_partial(columns, panel_rows)
+    shares = diagonal_partial(columns, panel_rows).reshape(4, 256, 256)
     shares = lax.all_to_all(shares, "zh", split_axis=0, concat_axis=0, tiled=True)
     summed = jnp.sum(shares.astype(jnp.float32), axis=0).astype(jnp.bfloat16)
-    mine, theirs = own_and_other((summed[:, :128], summed[:, 128:]))
-    summed = jnp.stack(own_and_other((move(mine, TURN), move(theirs, TURN_AND_SWAP))))
+    mine, theirs = ordered(sup, summed[:, :128], summed[:, 128:])
+    summed = jnp.stack(ordered(sup, move(mine, TURN), move(theirs, TURN_AND_PAIR)))
     diagonal_inverse = (pivot_inverse.astype(jnp.float32) - summed.astype(jnp.float32)).astype(jnp.bfloat16)
     return (panel_inverse, diagonal_inverse)
 

time: 190 us -> 184 us (0.968)
  the two profiles are of different devices: /device:TPU:14 before, /device:TPU:6 now
where the time goes in v5:
time: 184 us; the launch traced here: 182 us
  blocking collectives  68.6 us (37%)
  starting transfers between devices  44.4 us (24%)
  waiting for transfers between devices  34.5 us (19%)
  between operations  14.2 us (8%)
  Pallas kernels  12.3 us (7%)
  other arithmetic  6.16 us (3%)
    all_gather x1, blocking collectives, on_device(): lax.all_gather(masked_rows(turned, flags(x).astype(jnp.bfloat16)), 'zh')  34.9 us
    ppermute x7, starting transfers between devices, move(): return lax.ppermute(value, AXES, listed)  32.8 us
    ppermute x7, waiting for transfers between devices, move(): return lax.ppermute(value, AXES, listed)  21.3 us
    all_gather x1, blocking collectives, on_device(): block_parts = lax.all_gather(inverse_block.T, 'zl')  19.7 us
    all_gather x1, blocking collectives, on_device(): panel_rows = lax.all_gather(panel, 'x')  14 us
    all_to_all x1, waiting for transfers between devices, on_device(): lax.all_to_all(partial, 'x', split_axis=0, concat_axis=0, tiled=True)  8.52 us
    all_to_all x1, starting transfers between devices, on_device(): lax.all_to_all(shares, 'zh', split_axis=0, concat_axis=0, tiled=True)  6.56 us
    pallas_call x1, Pallas kernels, panel_partial(): pl.pallas_call(panel_kernel, grid=(groups,), in_specs=[pl.BlockSpec((1, p...  5.63 us
  transfers between devices with their start and end apart: 11, of which 7 were waited for; matrix products, arithmetic and copies ran while one was open for 4% of the time, Pallas kernels for 4%

profile of v5, /device:TPU:6, one launch (start us, length us, event | category | flops | bytes accessed | tf_op | source)
XLA Modules:
  0.0 181.9 jit_solution(1784700966190123867)
XLA Ops:
  7.2 19.7 %all-gather = bf16[768,384]{1,0:T(8,128)(2,1)} all-gather(bf16[192,384]{1,0:T(8,128)(2,1)} %bitcast.51), channel_id=2, replica_groups=mesh['zh'=4,'y'=4,'zl'=4,'x'=4,'core'=2] {'zl'}, dimensions={0}, use_global_device_ids=true | all-gather | bytes 737280 | tf_op jit(solution)/shard_map/all_gather | solution.py:140
  27.0 1.0 select_bitcast_fusion.4
  27.9 2.2 %collective-permute-start = (bf16[384,128]{1,0:T(8,128)(2,1)S(1)}, bf16[384,128]{1,0:T(8,128)(2,1)S(1)}, u32[]{:S(2)}, u32[]{:S(2)}) collective-permute-start(bf16[384,128]{1,0:T(8,128)(2,1)S(1)} %select_bitcast_fusion.4), channel_id=1, source_target_pairs={{0,8},{1,9},{2,10},{3,11},{4,12},{5,13},{6,14},{7,15},{8,0},{9,1},... | collective-permute-start | bytes 294920 | tf_op jit(solution)/shard_map/ppermute | solution.py:40
  30.1 1.4 convert_bitcast_fusion
  31.6 2.8 %collective-permute-done = bf16[384,128]{1,0:T(8,128)(2,1)S(1)} collective-permute-done((bf16[384,128]{1,0:T(8,128)(2,1)S(1)}, bf16[384,128]{1,0:T(8,128)(2,1)S(1)}, u32[]{:S(2)}, u32[]{:S(2)}) %collective-permute-start) | collective-permute-done | bytes 98336 | tf_op jit(solution)/shard_map/ppermute | solution.py:40
  34.4 1.0 bitcast_select_fusion.1
  35.4 0.1 broadcast_multiply_fusion
  35.5 2.7 %collective-permute-start.4 = (bf16[384,256]{1,0:T(8,128)(2,1)S(1)}, bf16[384,256]{1,0:T(8,128)(2,1)S(1)}, u32[]{:S(2)}, u32[]{:S(2)}) collective-permute-start(bf16[384,256]{1,0:T(8,128)(2,1)S(1)} %get-tuple-element.6), channel_id=1, source_target_pairs={{0,16},{1,17},{2,18},{3,19},{4,20},{5,21},{6,22},{7,23},{8,24},{9,... | collective-permute-start | bytes 589832 | tf_op jit(solution)/shard_map/ppermute | solution.py:40
  38.3 0.8 copy.9
  39.1 4.8 %collective-permute-start.1 = (bf16[384,256]{1,0:T(8,128)(2,1)S(1)}, bf16[384,256]{1,0:T(8,128)(2,1)S(1)}, u32[]{:S(2)}, u32[]{:S(2)}) collective-permute-start(bf16[384,256]{1,0:T(8,128)(2,1)S(1)} %get-tuple-element.7), channel_id=1, source_target_pairs={{0,0},{1,1},{2,32},{3,33},{4,64},{5,65},{6,96},{7,97},{8,8},{9,9},... | collective-permute-start | bytes 589832 | tf_op jit(solution)/shard_map/ppermute | solution.py:40
  44.0 1.8 %collective-permute-done.4 = bf16[384,256]{1,0:T(8,128)(2,1)S(1)} collective-permute-done((bf16[384,256]{1,0:T(8,128)(2,1)S(1)}, bf16[384,256]{1,0:T(8,128)(2,1)S(1)}, u32[]{:S(2)}, u32[]{:S(2)}) %collective-permute-start.4) | collective-permute-done | bytes 196640 | tf_op jit(solution)/shard_map/ppermute | solution.py:40
  45.8 0.8 pad_maximum_fusion
  46.6 5.6 %collective-permute-done.1.value_ref = bf16[384,256]{1,0:T(8,128)(2,1)S(1)} collective-permute-done((bf16[384,256]{1,0:T(8,128)(2,1)S(1)}, bf16[384,256]{1,0:T(8,128)(2,1)S(1)}, u32[]{:S(2)}, u32[]{:S(2)}) %collective-permute-start.1) | collective-permute-done | bytes 196640 | tf_op jit(solution)/shard_map/ppermute | solution.py:40
  52.2 0.7 copy-done.2
  52.9 1.8 shard_map.59
  54.7 34.9 %all-gather.2 = bf16[1536,256]{1,0:T(8,128)(2,1)} all-gather(bf16[384,256]{1,0:T(8,128)(2,1)} %shard_map.59), channel_id=4, replica_groups=mesh['zh'=4,'y'=4,'zl'=4,'x'=4,'core'=2] {'zh'}, dimensions={0}, use_global_device_ids=true | all-gather | bytes 983040 | tf_op jit(solution)/shard_map/all_gather | solution.py:144
  89.6 5.6 %shard_map.60 = bf16[4,384,256]{2,1,0:T(8,128)(2,1)} custom-call(bf16[4,2,4,192,384]{4,3,2,1,0:T(8,128)(2,1)} %bitcast.46, bf16[4,384,256]{2,1,0:T(8,128)(2,1)} %bitcast.47), custom_call_target="tpu_custom_call" | custom-call | flops 1207959552 | bytes 7340032 | tf_op jit(solution)/shard_map/pallas_call | solution.py:58
  95.2 5.0 %all-to-all-start = ((bf16[4,384,256]{2,1,0:T(8,128)(2,1)}), bf16[4,384,256]{2,1,0:T(8,128)(2,1)S(1)}, u32[]{:S(2)}, u32[]{:S(2)}) async-start(bf16[4,384,256]{2,1,0:T(8,128)(2,1)} %shard_map.60), calls=%async_computation | async-start | bytes 1572864 | tf_op jit(solution)/shard_map/all_to_all | solution.py:147
  100.3 8.5 %all-to-all-done = bf16[4,384,256]{2,1,0:T(8,128)(2,1)S(1)} async-done(((bf16[4,384,256]{2,1,0:T(8,128)(2,1)}), bf16[4,384,256]{2,1,0:T(8,128)(2,1)S(1)}, u32[]{:S(2)}, u32[]{:S(2)}) %all-to-all-start) | async-done | bytes 786464 | tf_op jit(solution)/shard_map/all_to_all | solution.py:147
  108.9 0.1 fusion.1
  109.0 14.0 %all_gather.36.right_ref = bf16[4,384,256]{2,1,0:T(8,128)(2,1)} all-gather(bf16[1,384,256]{2,1,0:T(8,128)(2,1)S(1)} %fusion.1), channel_id=1, replica_groups=mesh['zh'=4,'y'=4,'zl'=4,'x'=4,'core'=2] {'x'}, dimensions={0}, use_global_device_ids=true | all-gather | bytes 983040 | tf_op jit(solution)/shard_map/all_gather | solution.py:150
  123.1 4.9 %shard_map.61 = bf16[4,2,128,256]{3,2,1,0:T(8,128)(2,1)} custom-call(bf16[4,2,2,384,256]{4,3,2,1,0:T(8,128)(2,1)} %bitcast.48, bf16[4,384,256]{2,1,0:T(8,128)(2,1)} %all_gather.36.right_ref), custom_call_target="tpu_custom_call" | custom-call | flops 805306368 | bytes 5242880 | tf_op jit(solution)/shard_map/pallas_call | solution.py:89
  128.0 6.6 %all-to-all-start.1 = ((bf16[4,256,256]{2,1,0:T(8,128)(2,1)}), bf16[4,256,256]{2,1,0:T(8,128)(2,1)S(1)}, u32[]{:S(2)}, u32[]{:S(2)}) async-start(bf16[4,256,256]{2,1,0:T(8,128)(2,1)} %bitcast.50), calls=%async_computation.1 | async-start | bytes 1048576 | tf_op jit(solution)/shard_map/all_to_all | solution.py:155
  134.7 5.6 %collective-permute-start.2 = (bf16[384,128]{1,0:T(8,128)(2,1)S(1)}, bf16[384,128]{1,0:T(8,128)(2,1)S(1)}, u32[]{:S(2)}, u32[]{:S(2)}) collective-permute-start(bf16[384,128]{1,0:T(8,128)(2,1)S(1)} %get-tuple-element.10), channel_id=1, source_target_pairs={{0,0},{1,1},{2,32},{3,33},{4,64},{5,65},{6,96},{7,97},{8,8},{9,9},... | collective-permute-start | bytes 294920 | tf_op jit(solution)/shard_map/ppermute | solution.py:40
  140.3 6.9 %collective-permute-start.3 = (bf16[384,128]{1,0:T(8,128)(2,1)S(1)}, bf16[384,128]{1,0:T(8,128)(2,1)S(1)}, u32[]{:S(2)}, u32[]{:S(2)}) collective-permute-start(bf16[384,128]{1,0:T(8,128)(2,1)S(1)} %get-tuple-element.11), channel_id=1, source_target_pairs={{0,8},{1,9},{2,40},{3,41},{4,72},{5,73},{6,104},{7,105},{8,0},{9,1... | collective-permute-start | bytes 294920 | tf_op jit(solution)/shard_map/ppermute | solution.py:40
  147.3 6.9 %collective-permute-done.3 = bf16[384,128]{1,0:T(8,128)(2,1)S(1)} collective-permute-done((bf16[384,128]{1,0:T(8,128)(2,1)S(1)}, bf16[384,128]{1,0:T(8,128)(2,1)S(1)}, u32[]{:S(2)}, u32[]{:S(2)}) %collective-permute-start.3) | collective-permute-done | bytes 98336 | tf_op jit(solution)/shard_map/ppermute | solution.py:40
  154.2 4.7 %all-to-all-done.1 = bf16[4,256,256]{2,1,0:T(8,128)(2,1)S(1)} async-done(((bf16[4,256,256]{2,1,0:T(8,128)(2,1)}), bf16[4,256,256]{2,1,0:T(8,128)(2,1)S(1)}, u32[]{:S(2)}, u32[]{:S(2)}) %all-to-all-start.1) | async-done | bytes 524320 | tf_op jit(solution)/shard_map/all_to_all | solution.py:155
  159.0 5.0 %collective-permute-start.5 = (bf16[256,128]{1,0:T(8,128)(2,1)S(1)}, bf16[256,128]{1,0:T(8,128)(2,1)S(1)}, u32[]{:S(2)}, u32[]{:S(2)}) collective-permute-start(bf16[256,128]{1,0:T(8,128)(2,1)S(1)} %get-tuple-element.14), channel_id=1, source_target_pairs={{0,0},{1,1},{2,32},{3,33},{4,64},{5,65},{6,96},{7,97},{8,8},{9,9},... | collective-permute-start | bytes 196616 | tf_op jit(solution)/shard_map/ppermute | solution.py:40
  164.0 5.6 %collective-permute-start.6 = (bf16[256,128]{1,0:T(8,128)(2,1)S(1)}, bf16[256,128]{1,0:T(8,128)(2,1)S(1)}, u32[]{:S(2)}, u32[]{:S(2)}) collective-permute-start(bf16[256,128]{1,0:T(8,128)(2,1)S(1)} %get-tuple-element.15), channel_id=1, source_target_pairs={{0,8},{1,9},{2,40},{3,41},{4,72},{5,73},{6,104},{7,105},{8,0},{9,1... | collective-permute-start | bytes 196616 | tf_op jit(solution)/shard_map/ppermute | solution.py:40
  169.6 0.7 pad_maximum_fusion.2
  170.3 4.1 %collective-permute-done.6 = bf16[256,128]{1,0:T(8,128)(2,1)S(1)} collective-permute-done((bf16[256,128]{1,0:T(8,128)(2,1)S(1)}, bf16[256,128]{1,0:T(8,128)(2,1)S(1)}, u32[]{:S(2)}, u32[]{:S(2)}) %collective-permute-start.6) | collective-permute-done | bytes 65568 | tf_op jit(solution)/shard_map/ppermute | solution.py:40
  174.4 0.7 subtract_convert_fusion
  (25 shorter events, 0.8 us)
Async XLA Ops:
  7.2 82.4 %all-gather.7.cloned.1.call-start = ((), (), s32[]{:S(2)}) async-start(), calls=%async_computation.2 | async-start | bytes 5308416 | tf_op jit(solution)/shard_map/all_gather | solution.py:141
  26.9 96.2 %all-gather.9.cloned.1.call-start = ((), (), s32[]{:S(2)}) async-start(), calls=%async_computation.3 | async-start | bytes 3538944 | tf_op jit(solution)/shard_map/all_gather | solution.py:143
  27.9 6.5 %collective-permute-start = (bf16[384,128]{1,0:T(8,128)(2,1)S(1)}, bf16[384,128]{1,0:T(8,128)(2,1)S(1)}, u32[]{:S(2)}, u32[]{:S(2)}) collective-permute-start(bf16[384,128]{1,0:T(8,128)(2,1)S(1)} %select_bitcast_fusion.4), channel_id=1, source_target_pairs={{0,8},{1,9},{2,10},{3,11},{4,12},{5,13},{6,14},{7,15},{8,0},{9,1},... | collective-permute-start | bytes 294920 | tf_op jit(solution)/shard_map/ppermute | solution.py:40
  35.5 10.3 %collective-permute-start.4 = (bf16[384,256]{1,0:T(8,128)(2,1)S(1)}, bf16[384,256]{1,0:T(8,128)(2,1)S(1)}, u32[]{:S(2)}, u32[]{:S(2)}) collective-permute-start(bf16[384,256]{1,0:T(8,128)(2,1)S(1)} %get-tuple-element.6), channel_id=1, source_target_pairs={{0,16},{1,17},{2,18},{3,19},{4,20},{5,21},{6,22},{7,23},{8,24},{9,... | collective-permute-start | bytes 589832 | tf_op jit(solution)/shard_map/ppermute | solution.py:40
  39.1 13.1 %collective-permute-start.1 = (bf16[384,256]{1,0:T(8,128)(2,1)S(1)}, bf16[384,256]{1,0:T(8,128)(2,1)S(1)}, u32[]{:S(2)}, u32[]{:S(2)}) collective-permute-start(bf16[384,256]{1,0:T(8,128)(2,1)S(1)} %get-tuple-element.7), channel_id=1, source_target_pairs={{0,0},{1,1},{2,32},{3,33},{4,64},{5,65},{6,96},{7,97},{8,8},{9,9},... | collective-permute-start | bytes 589832 | tf_op jit(solution)/shard_map/ppermute | solution.py:40
  52.2 0.7 copy-start.2
  89.6 10.6 %copy-start.1 = (f32[3]{0:T(128)S(1)}, f32[3]{0:T(128)}, u32[]{:S(2)}) copy-start(f32[3]{0:T(128)} %get-tuple-element.17) | copy-start | bytes 40
  95.2 13.6 %all-to-all-start = ((bf16[4,384,256]{2,1,0:T(8,128)(2,1)}), bf16[4,384,256]{2,1,0:T(8,128)(2,1)S(1)}, u32[]{:S(2)}, u32[]{:S(2)}) async-start(bf16[4,384,256]{2,1,0:T(8,128)(2,1)} %shard_map.60), calls=%async_computation | async-start | bytes 1572864 | tf_op jit(solution)/shard_map/all_to_all | solution.py:147
  123.1 51.3 %copy-start = (bf16[2,256,128]{2,1,0:T(8,128)(2,1)S(1)}, bf16[2,256,128]{2,1,0:T(8,128)(2,1)}, u32[]{:S(2)}) copy-start(bf16[2,256,128]{2,1,0:T(8,128)(2,1)} %param.7) | copy-start | bytes 393220
  128.0 31.0 %all-to-all-start.1 = ((bf16[4,256,256]{2,1,0:T(8,128)(2,1)}), bf16[4,256,256]{2,1,0:T(8,128)(2,1)S(1)}, u32[]{:S(2)}, u32[]{:S(2)}) async-start(bf16[4,256,256]{2,1,0:T(8,128)(2,1)} %bitcast.50), calls=%async_computation.1 | async-start | bytes 1048576 | tf_op jit(solution)/shard_map/all_to_all | solution.py:155
  134.7 12.6 %collective-permute-start.2 = (bf16[384,128]{1,0:T(8,128)(2,1)S(1)}, bf16[384,128]{1,0:T(8,128)(2,1)S(1)}, u32[]{:S(2)}, u32[]{:S(2)}) collective-permute-start(bf16[384,128]{1,0:T(8,128)(2,1)S(1)} %get-tuple-element.10), channel_id=1, source_target_pairs={{0,0},{1,1},{2,32},{3,33},{4,64},{5,65},{6,96},{7,97},{8,8},{9,9},... | collective-permute-start | bytes 294920 | tf_op jit(solution)/shard_map/ppermute | solution.py:40
  140.3 13.9 %collective-permute-start.3 = (bf16[384,128]{1,0:T(8,128)(2,1)S(1)}, bf16[384,128]{1,0:T(8,128)(2,1)S(1)}, u32[]{:S(2)}, u32[]{:S(2)}) collective-permute-start(bf16[384,128]{1,0:T(8,128)(2,1)S(1)} %get-tuple-element.11), channel_id=1, source_target_pairs={{0,8},{1,9},{2,40},{3,41},{4,72},{5,73},{6,104},{7,105},{8,0},{9,1... | collective-permute-start | bytes 294920 | tf_op jit(solution)/shard_map/ppermute | solution.py:40
  159.0 11.2 %collective-permute-start.5 = (bf16[256,128]{1,0:T(8,128)(2,1)S(1)}, bf16[256,128]{1,0:T(8,128)(2,1)S(1)}, u32[]{:S(2)}, u32[]{:S(2)}) collective-permute-start(bf16[256,128]{1,0:T(8,128)(2,1)S(1)} %get-tuple-element.14), channel_id=1, source_target_pairs={{0,0},{1,1},{2,32},{3,33},{4,64},{5,65},{6,96},{7,97},{8,8},{9,9},... | collective-permute-start | bytes 196616 | tf_op jit(solution)/shard_map/ppermute | solution.py:40
  164.0 10.4 %collective-permute-start.6 = (bf16[256,128]{1,0:T(8,128)(2,1)S(1)}, bf16[256,128]{1,0:T(8,128)(2,1)S(1)}, u32[]{:S(2)}, u32[]{:S(2)}) collective-permute-start(bf16[256,128]{1,0:T(8,128)(2,1)S(1)} %get-tuple-element.15), channel_id=1, source_target_pairs={{0,8},{1,9},{2,40},{3,41},{4,72},{5,73},{6,104},{7,105},{8,0},{9,1... | collective-permute-start | bytes 196616 | tf_op jit(solution)/shard_map/ppermute | solution.py:40
Sparse Core Ops, SparseCore 0:
  27.0 44.4 all-gather.6
  73.6 36.2 all-gather.8

commit v6 on v5

--- a/solution.py
+++ b/solution.py
@@ -40,68 +40,16 @@
     return lax.ppermute(value, AXES, listed)
 
 
-def panel_kernel(block_ref, rows_ref, out_ref):
-    half = block_ref.shape[3]
-    total = jnp.zeros(out_ref.shape[1:], jnp.float32)
-    for group in range(4):
-        for part in range(2):
-            total += lax.dot_general(
-                block_ref[0, part, group], rows_ref[group, part * half : part * half + half, :],
-                CONTRACT_ROWS, preferred_element_type=jnp.float32,
-            )
-    out_ref[0] = total.astype(out_ref.dtype)
-
-
 def panel_partial(block, rows):
-    groups, parts, steps, half, height = block.shape
-    width = rows.shape[2]
-    return pl.pallas_call(
-        panel_kernel,
-        grid=(groups,),
-        in_specs=[
-            pl.BlockSpec((1, parts, steps, half, height), lambda g: (g, 0, 0, 0, 0)),
-            pl.BlockSpec(rows.shape, lambda g: (0, 0, 0)),
-        ],
-        out_specs=pl.BlockSpec((1, height, width), lambda g: (g, 0, 0)),
-        out_shape=jax.ShapeDtypeStruct((groups, height, width), jnp.bfloat16),
-        compiler_params=pltpu.CompilerParams(vmem_limit_bytes=VMEM_BYTES),
-        cost_estimate=pl.CostEstimate(
-            flops=4 * groups * steps * half * height * width,
-            bytes_accessed=7 * 1024 * 1024,
-            transcendentals=0,
-        ),
-    )(block, rows)
-
-
-def diagonal_kernel(left_ref, right_ref, out_ref):
-    total = jnp.zeros((256, 256), jnp.float32)
-    for group in range(4):
-        total += lax.dot_general(
-            left_ref[group, 0, 0], right_ref[group], CONTRACT_ROWS, preferred_element_type=jnp.float32
-        )
-    value = total.astype(out_ref.dtype)
-    out_ref[0, 0] = value[:128]
-    out_ref[1, 0] = value[128:]
+    rows = rows.reshape(rows.shape[0], 2, block.shape[3], rows.shape[2])
+    partial = jnp.einsum("ycztS,zctj->ySj", block, rows, preferred_element_type=jnp.float32)
+    return partial.astype(jnp.bfloat16)
 
 
 def diagonal_partial(left, right):
-    groups, cores, couples, depth, width = left.shape
-    return pl.pallas_call(
-        diagonal_kernel,
-        grid=(couples, cores),
-        in_specs=[
-            pl.BlockSpec((groups, 1, 1, depth, width), lambda p, c: (0, c, p, 0, 0)),
-            pl.BlockSpec(right.shape, lambda p, c: (0, 0, 0)),
-        ],
-        out_specs=pl.BlockSpec((2, 1, 128, 256), lambda p, c: (p, c, 0, 0)),
-        out_shape=jax.ShapeDtypeStruct((4, cores, 128, 256), jnp.bfloat16),
-        compiler_params=pltpu.CompilerParams(vmem_limit_bytes=VMEM_BYTES),
-        cost_estimate=pl.CostEstimate(
-            flops=2 * groups * cores * couples * depth * width * 256,
-            bytes_accessed=5 * 1024 * 1024,
-            transcendentals=0,
-        ),
-    )(left, right)
+    partial = jnp.einsum("gcpsi,gsj->pcij", left, right, preferred_element_type=jnp.float32)
+    partial = partial.astype(jnp.bfloat16).reshape(2, 2, 2, 128, 256)
+    return partial.transpose(0, 2, 1, 3, 4)
 
 
 def mask_kernel(value_ref, flag_ref, out_ref):

time: 184 us -> 183 us (level)
  Pallas kernels: 12.3 us -> 1.8 us
  matrix products: 0 us -> 8.03 us
  waiting for transfers between devices: 34.5 us -> 37.2 us
    pallas_call x2 -> x0, Pallas kernels: 10.5 us -> none  [the longest x1 5.63 us: panel_partial(): pl.pallas_call(panel_kernel, grid=(groups,), in_specs=[pl.BlockSpec((1, p...]
    dot_general x0 -> x2, matrix products: none -> 8.03 us  [the longest x1 4.8 us: panel_partial(): jnp.einsum('ycztS,zctj->ySj', block, rows, preferred_element_type=jnp.flo...]
    all_to_all x1, waiting for transfers between devices: 4.71 us -> 7.16 us  [on_device(): lax.all_to_all(shares, 'zh', split_axis=0, concat_axis=0, tiled=True)]
  transfers between devices with their start and end apart: 11 -> 11, of which waited for: 7 -> 7; matrix products, arithmetic and copies ran while one was open for 4% -> 6% of each run, Pallas kernels for 4% -> 1%
where the time goes in v6:
time: 183 us; the launch traced here: 181 us
  blocking collectives  67.3 us (37%)
  starting transfers between devices  43.4 us (24%)
  waiting for transfers between devices  37.2 us (20%)
  between operations  14.2 us (8%)
  matrix products  8.03 us (4%)
  other arithmetic  6.1 us (3%)
  local copies, waits for them, and re-layouts  2.86 us (2%)
    all_gather x1, blocking collectives, on_device(): lax.all_gather(masked_rows(turned, flags(x).astype(jnp.bfloat16)), 'zh')  34.4 us
    ppermute x7, starting transfers between devices, move(): return lax.ppermute(value, AXES, listed)  32 us
    ppermute x7, waiting for transfers between devices, move(): return lax.ppermute(value, AXES, listed)  20.4 us
    all_gather x1, blocking collectives, on_device(): block_parts = lax.all_gather(inverse_block.T, 'zl')  19.6 us
    all_gather x1, blocking collectives, on_device(): panel_rows = lax.all_gather(panel, 'x')  13.3 us
    all_to_all x1, waiting for transfers between devices, on_device(): lax.all_to_all(partial, 'x', split_axis=0, concat_axis=0, tiled=True)  9.56 us
    all_to_all x1, waiting for transfers between devices, on_device(): lax.all_to_all(shares, 'zh', split_axis=0, concat_axis=0, tiled=True)  7.16 us
    all_to_all x1, starting transfers between devices, on_device(): lax.all_to_all(shares, 'zh', split_axis=0, concat_axis=0, tiled=True)  6.67 us
  transfers between devices with their start and end apart: 11, of which 7 were waited for; matrix products, arithmetic and copies ran while one was open for 6% of the time, Pallas kernels for 1%

profile of v6, /device:TPU:6, one launch (start us, length us, event | category | flops | bytes accessed | tf_op | source)
XLA Modules:
  0.0 180.9 jit_solution(3110255751081435127)
XLA Ops:
  7.2 19.6 %all-gather.1 = bf16[768,384]{1,0:T(8,128)(2,1)} all-gather(bf16[192,384]{1,0:T(8,128)(2,1)} %bitcast.82), channel_id=3, replica_groups=mesh['zh'=4,'y'=4,'zl'=4,'x'=4,'core'=2] {'zl'}, dimensions={0}, use_global_device_ids=true | all-gather | bytes 737280 | tf_op jit(solution)/shard_map/all_gather | solution.py:88
  26.9 1.0 select_bitcast_fusion.4
  27.9 2.2 %collective-permute-start = (bf16[384,128]{1,0:T(8,128)(2,1)S(1)}, bf16[384,128]{1,0:T(8,128)(2,1)S(1)}, u32[]{:S(2)}, u32[]{:S(2)}) collective-permute-start(bf16[384,128]{1,0:T(8,128)(2,1)S(1)} %select_bitcast_fusion.4), channel_id=1, source_target_pairs={{0,8},{1,9},{2,10},{3,11},{4,12},{5,13},{6,14},{7,15},{8,0},{9,1},... | collective-permute-start | bytes 294920 | tf_op jit(solution)/shard_map/ppermute | solution.py:40
  30.1 1.4 convert_bitcast_fusion
  31.6 2.8 %collective-permute-done = bf16[384,128]{1,0:T(8,128)(2,1)S(1)} collective-permute-done((bf16[384,128]{1,0:T(8,128)(2,1)S(1)}, bf16[384,128]{1,0:T(8,128)(2,1)S(1)}, u32[]{:S(2)}, u32[]{:S(2)}) %collective-permute-start) | collective-permute-done | bytes 98336 | tf_op jit(solution)/shard_map/ppermute | solution.py:40
  34.4 1.0 bitcast_select_fusion.1
  35.5 2.7 %collective-permute-start.4 = (bf16[384,256]{1,0:T(8,128)(2,1)S(1)}, bf16[384,256]{1,0:T(8,128)(2,1)S(1)}, u32[]{:S(2)}, u32[]{:S(2)}) collective-permute-start(bf16[384,256]{1,0:T(8,128)(2,1)S(1)} %get-tuple-element.6), channel_id=1, source_target_pairs={{0,16},{1,17},{2,18},{3,19},{4,20},{5,21},{6,22},{7,23},{8,24},{9,... | collective-permute-start | bytes 589832 | tf_op jit(solution)/shard_map/ppermute | solution.py:40
  38.3 0.8 copy.29
  39.1 4.8 %collective-permute-start.1 = (bf16[384,256]{1,0:T(8,128)(2,1)S(1)}, bf16[384,256]{1,0:T(8,128)(2,1)S(1)}, u32[]{:S(2)}, u32[]{:S(2)}) collective-permute-start(bf16[384,256]{1,0:T(8,128)(2,1)S(1)} %get-tuple-element.7), channel_id=1, source_target_pairs={{0,0},{1,1},{2,32},{3,33},{4,64},{5,65},{6,96},{7,97},{8,8},{9,9},... | collective-permute-start | bytes 589832 | tf_op jit(solution)/shard_map/ppermute | solution.py:40
  44.0 1.8 %collective-permute-done.4 = bf16[384,256]{1,0:T(8,128)(2,1)S(1)} collective-permute-done((bf16[384,256]{1,0:T(8,128)(2,1)S(1)}, bf16[384,256]{1,0:T(8,128)(2,1)S(1)}, u32[]{:S(2)}, u32[]{:S(2)}) %collective-permute-start.4) | collective-permute-done | bytes 196640 | tf_op jit(solution)/shard_map/ppermute | solution.py:40
  45.8 0.8 pad_maximum_fusion
  46.7 5.5 %collective-permute-done.1.value_ref = bf16[384,256]{1,0:T(8,128)(2,1)S(1)} collective-permute-done((bf16[384,256]{1,0:T(8,128)(2,1)S(1)}, bf16[384,256]{1,0:T(8,128)(2,1)S(1)}, u32[]{:S(2)}, u32[]{:S(2)}) %collective-permute-start.1) | collective-permute-done | bytes 196640 | tf_op jit(solution)/shard_map/ppermute | solution.py:40
  52.2 0.7 copy-done.2
  52.9 1.8 shard_map.59
  54.7 34.4 %all-gather = bf16[1536,256]{1,0:T(8,128)(2,1)S(1)} all-gather(bf16[384,256]{1,0:T(8,128)(2,1)} %shard_map.59), channel_id=2, replica_groups=mesh['zh'=4,'y'=4,'zl'=4,'x'=4,'core'=2] {'zh'}, dimensions={0}, use_global_device_ids=true | all-gather | bytes 983040 | tf_op jit(solution)/shard_map/all_gather | solution.py:92
  89.1 4.8 %fusion.5 = bf16[4,384,256]{1,2,0:T(8,128)(2,1)} fusion(bf16[4,2,192,256,1]{3,2,1,4,0:T(8,128)(2,1)S(1)} %bitcast.80, bf16[4,2,4,192,384]{4,3,2,1,0:T(8,128)(2,1)} %bitcast.85), kind=kOutput, calls=%fused_computation.6 | convolution fusion | flops 1208352768 | bytes 6291456 | tf_op jit(solution)/shard_map/ycztS,zctj->ySj/dot_general | solution.py:45
  93.9 4.6 %all-to-all-start = ((bf16[4,384,256]{1,2,0:T(8,128)(2,1)}), bf16[4,384,256]{1,2,0:T(8,128)(2,1)S(1)}, u32[]{:S(2)}, u32[]{:S(2)}) async-start(bf16[4,384,256]{1,2,0:T(8,128)(2,1)} %fusion.5), calls=%async_computation | async-start | bytes 1572864 | tf_op jit(solution)/shard_map/all_to_all | solution.py:95
  98.5 9.6 %all-to-all-done = bf16[4,384,256]{1,2,0:T(8,128)(2,1)S(1)} async-done(((bf16[4,384,256]{1,2,0:T(8,128)(2,1)}), bf16[4,384,256]{1,2,0:T(8,128)(2,1)S(1)}, u32[]{:S(2)}, u32[]{:S(2)}) %all-to-all-start) | async-done | bytes 786464 | tf_op jit(solution)/shard_map/all_to_all | solution.py:95
  108.4 13.3 %all_gather.34 = bf16[4,384,256]{2,1,0:T(8,128)(2,1)S(1)} all-gather(bf16[1,384,256]{2,1,0:T(8,128)(2,1)S(1)} %copy.19), channel_id=1, replica_groups=mesh['zh'=4,'y'=4,'zl'=4,'x'=4,'core'=2] {'x'}, dimensions={0}, use_global_device_ids=true | all-gather | bytes 983040 | tf_op jit(solution)/shard_map/all_gather | solution.py:98
  121.7 3.2 %fusion.4 = bf16[256,2,2,256]{0,3,2,1:T(8,128)(2,1)S(1)} fusion(bf16[4,2,2,384,256]{4,3,2,1,0:T(8,128)(2,1)} %bitcast.86, bf16[4,384,256]{2,1,0:T(8,128)(2,1)S(1)} %all_gather.34), kind=kOutput, calls=%fused_computation.5 | convolution fusion | flops 805568512 | bytes 4456448 | tf_op jit(solution)/shard_map/gcpsi,gsj->pcij/dot_general | solution.py:50
  124.9 0.8 copy.21
  125.8 6.7 %all-to-all-start.1 = ((bf16[4,256,256]{2,1,0:T(8,128)(2,1)}), bf16[4,256,256]{2,1,0:T(8,128)(2,1)S(1)}, u32[]{:S(2)}, u32[]{:S(2)}) async-start(bf16[4,256,256]{2,1,0:T(8,128)(2,1)} %bitcast.29), calls=%async_computation.1 | async-start | bytes 1048576 | tf_op jit(solution)/shard_map/all_to_all | solution.py:103
  132.5 0.2 copy.18
  132.8 6.3 %collective-permute-start.2 = (bf16[384,128]{1,0:T(8,128)(2,1)S(1)}, bf16[384,128]{1,0:T(8,128)(2,1)S(1)}, u32[]{:S(2)}, u32[]{:S(2)}) collective-permute-start(bf16[384,128]{1,0:T(8,128)(2,1)S(1)} %get-tuple-element.10), channel_id=1, source_target_pairs={{0,0},{1,1},{2,32},{3,33},{4,64},{5,65},{6,96},{7,97},{8,8},{9,9},... | collective-permute-start | bytes 294920 | tf_op jit(solution)/shard_map/ppermute | solution.py:40
  139.0 5.6 %collective-permute-start.3 = (bf16[384,128]{1,0:T(8,128)(2,1)S(1)}, bf16[384,128]{1,0:T(8,128)(2,1)S(1)}, u32[]{:S(2)}, u32[]{:S(2)}) collective-permute-start(bf16[384,128]{1,0:T(8,128)(2,1)S(1)} %get-tuple-element.11), channel_id=1, source_target_pairs={{0,8},{1,9},{2,40},{3,41},{4,72},{5,73},{6,104},{7,105},{8,0},{9,1... | collective-permute-start | bytes 294920 | tf_op jit(solution)/shard_map/ppermute | solution.py:40
  144.7 7.0 %collective-permute-done.3 = bf16[384,128]{1,0:T(8,128)(2,1)S(1)} collective-permute-done((bf16[384,128]{1,0:T(8,128)(2,1)S(1)}, bf16[384,128]{1,0:T(8,128)(2,1)S(1)}, u32[]{:S(2)}, u32[]{:S(2)}) %collective-permute-start.3) | collective-permute-done | bytes 98336 | tf_op jit(solution)/shard_map/ppermute | solution.py:40
  151.7 7.2 %all-to-all-done.1 = bf16[4,256,256]{2,1,0:T(8,128)(2,1)S(1)} async-done(((bf16[4,256,256]{2,1,0:T(8,128)(2,1)}), bf16[4,256,256]{2,1,0:T(8,128)(2,1)S(1)}, u32[]{:S(2)}, u32[]{:S(2)}) %all-to-all-start.1) | async-done | bytes 524320 | tf_op jit(solution)/shard_map/all_to_all | solution.py:103
  158.9 4.0 %collective-permute-start.5 = (bf16[256,128]{1,0:T(8,128)(2,1)S(1)}, bf16[256,128]{1,0:T(8,128)(2,1)S(1)}, u32[]{:S(2)}, u32[]{:S(2)}) collective-permute-start(bf16[256,128]{1,0:T(8,128)(2,1)S(1)} %get-tuple-element.14), channel_id=1, source_target_pairs={{0,0},{1,1},{2,32},{3,33},{4,64},{5,65},{6,96},{7,97},{8,8},{9,9},... | collective-permute-start | bytes 196616 | tf_op jit(solution)/shard_map/ppermute | solution.py:40
  162.9 6.4 %collective-permute-start.6 = (bf16[256,128]{1,0:T(8,128)(2,1)S(1)}, bf16[256,128]{1,0:T(8,128)(2,1)S(1)}, u32[]{:S(2)}, u32[]{:S(2)}) collective-permute-start(bf16[256,128]{1,0:T(8,128)(2,1)S(1)} %get-tuple-element.15), channel_id=1, source_target_pairs={{0,8},{1,9},{2,40},{3,41},{4,72},{5,73},{6,104},{7,105},{8,0},{9,1... | collective-permute-start | bytes 196616 | tf_op jit(solution)/shard_map/ppermute | solution.py:40
  169.3 0.7 pad_maximum_fusion.2
  170.0 3.3 %collective-permute-done.6 = bf16[256,128]{1,0:T(8,128)(2,1)S(1)} collective-permute-done((bf16[256,128]{1,0:T(8,128)(2,1)S(1)}, bf16[256,128]{1,0:T(8,128)(2,1)S(1)}, u32[]{:S(2)}, u32[]{:S(2)}) %collective-permute-start.6) | collective-permute-done | bytes 65568 | tf_op jit(solution)/shard_map/ppermute | solution.py:40
  173.3 0.7 subtract_convert_fusion
  (28 shorter events, 1.1 us)
Async XLA Ops:
  7.2 81.9 %all-gather.7.cloned.1.call-start = ((), (), s32[]{:S(2)}) async-start(), calls=%async_computation.2 | async-start | bytes 5308416 | tf_op jit(solution)/shard_map/all_gather | solution.py:89
  26.9 94.8 %all-gather.9.cloned.1.call-start = ((), (), s32[]{:S(2)}) async-start(), calls=%async_computation.3 | async-start | bytes 3538944 | tf_op jit(solution)/shard_map/all_gather | solution.py:91
  27.9 6.5 %collective-permute-start = (bf16[384,128]{1,0:T(8,128)(2,1)S(1)}, bf16[384,128]{1,0:T(8,128)(2,1)S(1)}, u32[]{:S(2)}, u32[]{:S(2)}) collective-permute-start(bf16[384,128]{1,0:T(8,128)(2,1)S(1)} %select_bitcast_fusion.4), channel_id=1, source_target_pairs={{0,8},{1,9},{2,10},{3,11},{4,12},{5,13},{6,14},{7,15},{8,0},{9,1},... | collective-permute-start | bytes 294920 | tf_op jit(solution)/shard_map/ppermute | solution.py:40
  35.5 10.3 %collective-permute-start.4 = (bf16[384,256]{1,0:T(8,128)(2,1)S(1)}, bf16[384,256]{1,0:T(8,128)(2,1)S(1)}, u32[]{:S(2)}, u32[]{:S(2)}) collective-permute-start(bf16[384,256]{1,0:T(8,128)(2,1)S(1)} %get-tuple-element.6), channel_id=1, source_target_pairs={{0,16},{1,17},{2,18},{3,19},{4,20},{5,21},{6,22},{7,23},{8,24},{9,... | collective-permute-start | bytes 589832 | tf_op jit(solution)/shard_map/ppermute | solution.py:40
  39.1 13.1 %collective-permute-start.1 = (bf16[384,256]{1,0:T(8,128)(2,1)S(1)}, bf16[384,256]{1,0:T(8,128)(2,1)S(1)}, u32[]{:S(2)}, u32[]{:S(2)}) collective-permute-start(bf16[384,256]{1,0:T(8,128)(2,1)S(1)} %get-tuple-element.7), channel_id=1, source_target_pairs={{0,0},{1,1},{2,32},{3,33},{4,64},{5,65},{6,96},{7,97},{8,8},{9,9},... | collective-permute-start | bytes 589832 | tf_op jit(solution)/shard_map/ppermute | solution.py:40
  52.2 0.7 copy-start.2
  89.1 9.4 %copy-start.1 = (f32[3]{0:T(128)S(1)}, f32[3]{0:T(128)}, u32[]{:S(2)}) copy-start(f32[3]{0:T(128)} %get-tuple-element.17) | copy-start | bytes 40
  93.9 14.2 %all-to-all-start = ((bf16[4,384,256]{1,2,0:T(8,128)(2,1)}), bf16[4,384,256]{1,2,0:T(8,128)(2,1)S(1)}, u32[]{:S(2)}, u32[]{:S(2)}) async-start(bf16[4,384,256]{1,2,0:T(8,128)(2,1)} %fusion.5), calls=%async_computation | async-start | bytes 1572864 | tf_op jit(solution)/shard_map/all_to_all | solution.py:95
  124.9 48.4 %copy-start = (bf16[2,256,128]{2,1,0:T(8,128)(2,1)S(1)}, bf16[2,256,128]{2,1,0:T(8,128)(2,1)}, u32[]{:S(2)}) copy-start(bf16[2,256,128]{2,1,0:T(8,128)(2,1)} %param.7) | copy-start | bytes 393220
  125.8 33.0 %all-to-all-start.1 = ((bf16[4,256,256]{2,1,0:T(8,128)(2,1)}), bf16[4,256,256]{2,1,0:T(8,128)(2,1)S(1)}, u32[]{:S(2)}, u32[]{:S(2)}) async-start(bf16[4,256,256]{2,1,0:T(8,128)(2,1)} %bitcast.29), calls=%async_computation.1 | async-start | bytes 1048576 | tf_op jit(solution)/shard_map/all_to_all | solution.py:103
  132.8 11.9 %collective-permute-start.2 = (bf16[384,128]{1,0:T(8,128)(2,1)S(1)}, bf16[384,128]{1,0:T(8,128)(2,1)S(1)}, u32[]{:S(2)}, u32[]{:S(2)}) collective-permute-start(bf16[384,128]{1,0:T(8,128)(2,1)S(1)} %get-tuple-element.10), channel_id=1, source_target_pairs={{0,0},{1,1},{2,32},{3,33},{4,64},{5,65},{6,96},{7,97},{8,8},{9,9},... | collective-permute-start | bytes 294920 | tf_op jit(solution)/shard_map/ppermute | solution.py:40
  139.0 12.6 %collective-permute-start.3 = (bf16[384,128]{1,0:T(8,128)(2,1)S(1)}, bf16[384,128]{1,0:T(8,128)(2,1)S(1)}, u32[]{:S(2)}, u32[]{:S(2)}) collective-permute-start(bf16[384,128]{1,0:T(8,128)(2,1)S(1)} %get-tuple-element.11), channel_id=1, source_target_pairs={{0,8},{1,9},{2,40},{3,41},{4,72},{5,73},{6,104},{7,105},{8,0},{9,1... | collective-permute-start | bytes 294920 | tf_op jit(solution)/shard_map/ppermute | solution.py:40
  158.9 11.1 %collective-permute-start.5 = (bf16[256,128]{1,0:T(8,128)(2,1)S(1)}, bf16[256,128]{1,0:T(8,128)(2,1)S(1)}, u32[]{:S(2)}, u32[]{:S(2)}) collective-permute-start(bf16[256,128]{1,0:T(8,128)(2,1)S(1)} %get-tuple-element.14), channel_id=1, source_target_pairs={{0,0},{1,1},{2,32},{3,33},{4,64},{5,65},{6,96},{7,97},{8,8},{9,9},... | collective-permute-start | bytes 196616 | tf_op jit(solution)/shard_map/ppermute | solution.py:40
  162.9 10.4 %collective-permute-start.6 = (bf16[256,128]{1,0:T(8,128)(2,1)S(1)}, bf16[256,128]{1,0:T(8,128)(2,1)S(1)}, u32[]{:S(2)}, u32[]{:S(2)}) collective-permute-start(bf16[256,128]{1,0:T(8,128)(2,1)S(1)} %get-tuple-element.15), channel_id=1, source_target_pairs={{0,8},{1,9},{2,40},{3,41},{4,72},{5,73},{6,104},{7,105},{8,0},{9,1... | collective-permute-start | bytes 196616 | tf_op jit(solution)/shard_map/ppermute | solution.py:40
Sparse Core Ops, SparseCore 0:
  27.0 44.4 all-gather.6
  73.6 36.2 all-gather.8

commit v7 on v6

--- a/solution.py
+++ b/solution.py
@@ -1,16 +1,12 @@
 import jax
 import jax.numpy as jnp
 from jax import lax
-from jax.experimental import pallas as pl
-from jax.experimental.pallas import tpu as pltpu
 from jax.sharding import Mesh, PartitionSpec as P
 
 SUPERNODES = 2
 TILE = 128
 AXES = ("zh", "y", "zl", "x", "core")
 SIZES = (4, 4, 4, 4, 2)
-CONTRACT_ROWS = (((0,), (0,)), ((), ()))
-VMEM_BYTES = 60 * 1024 * 1024
 
 
 def pairs(move):
@@ -30,6 +26,7 @@
     return listed
 
 
+BOTH_WAYS = [[0, 2, 4, 6], [7, 5, 3, 1]]
 PAIR = pairs(lambda zh, y, zl, x, core: (zh, y, zl ^ 1, x, core))
 CROSS = pairs(lambda zh, y, zl, x, core: (zh, y, zl ^ 2, x, core))
 TURN = pairs(lambda zh, y, zl, x, core: (zh, x, zl, y, core))
@@ -52,19 +49,6 @@
     return partial.transpose(0, 2, 1, 3, 4)
 
 
-def mask_kernel(value_ref, flag_ref, out_ref):
-    out_ref[...] = value_ref[...] * flag_ref[...]
-
-
-def masked_rows(value, flag):
-    return pl.pallas_call(
-        mask_kernel,
-        out_shape=jax.ShapeDtypeStruct(value.shape, value.dtype),
-        compiler_params=pltpu.CompilerParams(vmem_limit_bytes=VMEM_BYTES),
-        cost_estimate=pl.CostEstimate(flops=400 * 10**9, bytes_accessed=10**6, transcendentals=0),
-    )(value, flag)
-
-
 def on_device(inverse_block, panels, structure, pivot_inverse):
     zh, y, zl, x = (lax.axis_index(name) for name in ("zh", "y", "zl", "x"))
     sup = lax.rem(zl, 2)
@@ -81,15 +65,17 @@
         return jnp.where(first, mine, theirs), jnp.where(first, theirs, mine)
 
     mine, theirs = ordered(sup, panels[0], panels[1])
-    wide = jnp.concatenate(ordered(sup, mine, move(theirs, PAIR)), axis=1)
+    block_parts = lax.all_gather(inverse_block.T, "zl")
+    theirs, block_parts = lax.optimization_barrier((move(theirs, PAIR), block_parts))
+    wide = jnp.concatenate(ordered(sup, mine, theirs), axis=1)
+    wide = wide * flags(y).astype(jnp.bfloat16)
     turned = move(wide, TURN)
-    wide = wide * flags(y).astype(jnp.bfloat16)
 
-    block_parts = lax.all_gather(inverse_block.T, "zl")
     block = lax.all_gather(block_parts, ("y", "core")).reshape((4, 2) + block_parts.shape)
     panel_parts = jnp.stack(ordered(zl // 2, wide, move(wide, CROSS)))
+    turned, panel_parts = lax.optimization_barrier((turned, panel_parts))
     columns = lax.all_gather(panel_parts, ("y", "core")).reshape((4, 2) + panel_parts.shape)
-    rows = lax.all_gather(masked_rows(turned, flags(x).astype(jnp.bfloat16)), "zh")
+    rows = lax.all_gather(turned, "zh")
 
     partial = panel_partial(block, rows)
     parts = lax.all_to_all(partial, "x", split_axis=0, concat_axis=0, tiled=True)
@@ -97,13 +83,18 @@
     panel = (-(jnp.sum(parts.astype(jnp.float32), axis=0) * weight)).astype(jnp.bfloat16)
     panel_rows = lax.all_gather(panel, "x")
     mine, theirs = ordered(sup, panel[:, :128], panel[:, 128:])
-    panel_inverse = jnp.stack(ordered(sup, move(mine, TURN), move(theirs, TURN_AND_PAIR)))
+    panel_moved = move(mine, TURN), move(theirs, TURN_AND_PAIR)
 
     shares = diagonal_partial(columns, panel_rows).reshape(4, 256, 256)
-    shares = lax.all_to_all(shares, "zh", split_axis=0, concat_axis=0, tiled=True)
+    shares = jnp.where(lax.axis_index("core") == 0, shares, shares[::-1])
+    shares = lax.all_to_all(
+        shares, ("zh", "core"), split_axis=0, concat_axis=0, tiled=True, axis_index_groups=BOTH_WAYS
+    )
     summed = jnp.sum(shares.astype(jnp.float32), axis=0).astype(jnp.bfloat16)
     mine, theirs = ordered(sup, summed[:, :128], summed[:, 128:])
-    summed = jnp.stack(ordered(sup, move(mine, TURN), move(theirs, TURN_AND_PAIR)))
+    summed = move(mine, TURN), move(theirs, TURN_AND_PAIR)
+    panel_inverse = jnp.stack(ordered(sup, *panel_moved))
+    summed = jnp.stack(ordered(sup, *summed))
     diagonal_inverse = (pivot_inverse.astype(jnp.float32) - summed.astype(jnp.float32)).astype(jnp.bfloat16)
     return (panel_inverse, diagonal_inverse)
 

time: 183 us -> 182 us (level)
  local copies, waits for them, and re-layouts: 2.86 us -> 0.18 us
  waiting for transfers between devices: 37.2 us -> 39.7 us
    ppermute x7, waiting for transfers between devices: 20.4 us -> 29.3 us  [move(): return lax.ppermute(value, AXES, listed)]
    all_to_all x1, waiting for transfers between devices: 7.16 us -> 0.8 us  [on_device(): lax.all_to_all(shares, ('zh', 'core'), split_axis=0, concat_axis=0, tiled...]
    all_gather x1, blocking collectives: 19.6 us -> 17.5 us  [on_device(): block_parts = lax.all_gather(inverse_block.T, 'zl')]
  transfers between devices with their start and end apart: 11 -> 11, of which waited for: 7 -> 7; matrix products, arithmetic and copies ran while one was open for 6% -> 5% of each run, Pallas kernels for 1% -> 0%
where the time goes in v7:
time: 182 us; the launch traced here: 180 us
  blocking collectives  66.7 us (37%)
  starting transfers between devices  44.9 us (25%)
  waiting for transfers between devices  39.7 us (22%)
  between operations  14.2 us (8%)
  matrix products  7.95 us (4%)
  other arithmetic  6.51 us (4%)
    all_gather x1, blocking collectives, on_device(): rows = lax.all_gather(turned, 'zh')  35.9 us
    ppermute x7, starting transfers between devices, move(): return lax.ppermute(value, AXES, listed)  31.9 us
    ppermute x7, waiting for transfers between devices, move(): return lax.ppermute(value, AXES, listed)  29.3 us
    all_gather x1, blocking collectives, on_device(): block_parts = lax.all_gather(inverse_block.T, 'zl')  17.5 us
    all_gather x1, blocking collectives, on_device(): panel_rows = lax.all_gather(panel, 'x')  13.3 us
    all_to_all x1, waiting for transfers between devices, on_device(): lax.all_to_all(partial, 'x', split_axis=0, concat_axis=0, tiled=True)  9.57 us
    all_to_all x1, starting transfers between devices, on_device(): lax.all_to_all(shares, ('zh', 'core'), split_axis=0, concat_axis=0, tiled...  8.15 us
    all_to_all x1, starting transfers between devices, on_device(): lax.all_to_all(partial, 'x', split_axis=0, concat_axis=0, tiled=True)  4.8 us
  transfers between devices with their start and end apart: 11, of which 7 were waited for; matrix products, arithmetic and copies ran while one was open for 5% of the time, Pallas kernels for 0%

profile of v7, /device:TPU:6, one launch (start us, length us, event | category | flops | bytes accessed | tf_op | source)
XLA Modules:
  0.0 180.2 jit_solution(11626724255966519926)
XLA Ops:
  7.2 1.0 select_bitcast_fusion.4
  8.2 3.8 %collective-permute-start = (bf16[384,128]{1,0:T(8,128)(2,1)S(1)}, bf16[384,128]{1,0:T(8,128)(2,1)S(1)}, u32[]{:S(2)}, u32[]{:S(2)}) collective-permute-start(bf16[384,128]{1,0:T(8,128)(2,1)S(1)} %select_bitcast_fusion.4), channel_id=1, source_target_pairs={{0,8},{1,9},{2,10},{3,11},{4,12},{5,13},{6,14},{7,15},{8,0},{9,1},... | collective-permute-start | bytes 294920 | tf_op jit(solution)/shard_map/ppermute | solution.py:37
  12.0 17.5 %all-gather = bf16[768,384]{1,0:T(8,128)(2,1)} all-gather(bf16[192,384]{1,0:T(8,128)(2,1)} %bitcast.73), channel_id=2, replica_groups=mesh['zh'=4,'y'=4,'zl'=4,'x'=4,'core'=2] {'zl'}, dimensions={0}, use_global_device_ids=true | all-gather | bytes 737280 | tf_op jit(solution)/shard_map/all_gather | solution.py:68
  29.6 0.8 convert_bitcast_fusion
  30.5 1.0 bitcast_select_fusion.1
  31.5 0.1 maximum_multiply_fusion
  31.6 2.7 %collective-permute-start.2 = (bf16[384,256]{1,0:T(8,128)(2,1)S(1)}, bf16[384,256]{1,0:T(8,128)(2,1)S(1)}, u32[]{:S(2)}, u32[]{:S(2)}) collective-permute-start(bf16[384,256]{1,0:T(8,128)(2,1)S(1)} %maximum_multiply_fusion), channel_id=1, source_target_pairs={{0,16},{1,17},{2,18},{3,19},{4,20},{5,21},{6,22},{7,23},{8,24},{9,... | collective-permute-start | bytes 589832 | tf_op jit(solution)/shard_map/ppermute | solution.py:37
  34.3 4.8 %collective-permute-start.1 = (bf16[384,256]{1,0:T(8,128)(2,1)S(1)}, bf16[384,256]{1,0:T(8,128)(2,1)S(1)}, u32[]{:S(2)}, u32[]{:S(2)}) collective-permute-start(bf16[384,256]{1,0:T(8,128)(2,1)S(1)} %maximum_multiply_fusion), channel_id=1, source_target_pairs={{0,0},{1,1},{2,32},{3,33},{4,64},{5,65},{6,96},{7,97},{8,8},{9,9},... | collective-permute-start | bytes 589832 | tf_op jit(solution)/shard_map/ppermute | solution.py:37
  39.1 2.9 %collective-permute-done.2 = bf16[384,256]{1,0:T(8,128)(2,1)S(1)} collective-permute-done((bf16[384,256]{1,0:T(8,128)(2,1)S(1)}, bf16[384,256]{1,0:T(8,128)(2,1)S(1)}, u32[]{:S(2)}, u32[]{:S(2)}) %collective-permute-start.2) | collective-permute-done | bytes 196640 | tf_op jit(solution)/shard_map/ppermute | solution.py:37
  42.1 0.8 pad_maximum_fusion
  42.9 4.6 %collective-permute-done.1 = bf16[384,256]{1,0:T(8,128)(2,1)S(1)} collective-permute-done((bf16[384,256]{1,0:T(8,128)(2,1)S(1)}, bf16[384,256]{1,0:T(8,128)(2,1)S(1)}, u32[]{:S(2)}, u32[]{:S(2)}) %collective-permute-start.1) | collective-permute-done | bytes 196640 | tf_op jit(solution)/shard_map/ppermute | solution.py:37
  47.6 35.9 %all-gather.2 = bf16[1536,256]{1,0:T(8,128)(2,1)S(1)} all-gather(bf16[384,256]{1,0:T(8,128)(2,1)S(1)} %collective-permute-done.1), channel_id=4, replica_groups=mesh['zh'=4,'y'=4,'zl'=4,'x'=4,'core'=2] {'zh'}, dimensions={0}, use_global_device_ids=true | all-gather | bytes 983040 | tf_op jit(solution)/shard_map/all_gather | solution.py:78
  83.5 4.7 %bitcast_convert_fusion = bf16[4,384,256]{2,1,0:T(8,128)(2,1)} fusion(bf16[4,2,4,192,384]{4,3,2,1,0:T(8,128)(2,1)} %bitcast.74, bf16[4,2,192,256,1]{3,2,1,0,4:T(8,128)(2,1)S(1)} %bitcast.71), kind=kOutput, calls=%fused_computation | convolution fusion | flops 1208352768 | bytes 6291456 | tf_op jit(solution)/shard_map/ycztS,zctj->ySj/dot_general | solution.py:42
  88.2 4.8 %all-to-all-start = ((bf16[4,384,256]{2,1,0:T(8,128)(2,1)}), bf16[4,384,256]{2,1,0:T(8,128)(2,1)S(1)}, u32[]{:S(2)}, u32[]{:S(2)}) async-start(bf16[4,384,256]{2,1,0:T(8,128)(2,1)} %bitcast_convert_fusion), calls=%async_computation | async-start | bytes 1572864 | tf_op jit(solution)/shard_map/all_to_all | solution.py:81
  93.1 9.6 %all-to-all-done = bf16[4,384,256]{2,1,0:T(8,128)(2,1)S(1)} async-done(((bf16[4,384,256]{2,1,0:T(8,128)(2,1)}), bf16[4,384,256]{2,1,0:T(8,128)(2,1)S(1)}, u32[]{:S(2)}, u32[]{:S(2)}) %all-to-all-start) | async-done | bytes 786464 | tf_op jit(solution)/shard_map/all_to_all | solution.py:81
  102.7 0.1 convert_reduce_fusion
  102.8 0.1 fusion.5
  102.9 13.3 %all_gather.34 = bf16[4,384,256]{2,1,0:T(8,128)(2,1)S(1)} all-gather(bf16[1,384,256]{2,1,0:T(8,128)(2,1)S(1)} %fusion.5), channel_id=1, replica_groups=mesh['zh'=4,'y'=4,'zl'=4,'x'=4,'core'=2] {'x'}, dimensions={0}, use_global_device_ids=true | all-gather | bytes 983040 | tf_op jit(solution)/shard_map/all_gather | solution.py:84
  116.2 3.2 %fusion = bf16[256,2,2,256]{0,3,2,1:T(8,128)(2,1)S(1)} fusion(bf16[4,2,2,384,256]{4,3,2,1,0:T(8,128)(2,1)} %bitcast.75, bf16[4,384,256]{2,1,0:T(8,128)(2,1)S(1)} %all_gather.34), kind=kOutput, calls=%fused_computation.3 | convolution fusion | flops 805568512 | bytes 4456448 | tf_op jit(solution)/shard_map/gcpsi,gsj->pcij/dot_general | solution.py:47
  119.5 0.9 reverse_select_fusion
  120.4 8.1 %all-to-all-start.1 = ((bf16[4,256,256]{2,1,0:T(8,128)(2,1)}), bf16[4,256,256]{2,1,0:T(8,128)(2,1)S(1)}, u32[]{:S(2)}, u32[]{:S(2)}) async-start(bf16[4,256,256]{2,1,0:T(8,128)(2,1)} %reverse_select_fusion), calls=%async_computation.1 | async-start | bytes 1048576 | tf_op jit(solution)/shard_map/all_to_all | solution.py:90
  128.6 0.1 negate_convert_fusion
  128.7 3.8 %collective-permute-start.3 = (bf16[384,128]{1,0:T(8,128)(2,1)S(1)}, bf16[384,128]{1,0:T(8,128)(2,1)S(1)}, u32[]{:S(2)}, u32[]{:S(2)}) collective-permute-start(bf16[384,128]{1,0:T(8,128)(2,1)S(1)} %get-tuple-element.16), channel_id=1, source_target_pairs={{0,0},{1,1},{2,32},{3,33},{4,64},{5,65},{6,96},{7,97},{8,8},{9,9},... | collective-permute-start | bytes 294920 | tf_op jit(solution)/shard_map/ppermute | solution.py:37
  132.5 5.4 %collective-permute-start.4 = (bf16[384,128]{1,0:T(8,128)(2,1)S(1)}, bf16[384,128]{1,0:T(8,128)(2,1)S(1)}, u32[]{:S(2)}, u32[]{:S(2)}) collective-permute-start(bf16[384,128]{1,0:T(8,128)(2,1)S(1)} %get-tuple-element.17), channel_id=1, source_target_pairs={{0,8},{1,9},{2,40},{3,41},{4,72},{5,73},{6,104},{7,105},{8,0},{9,1... | collective-permute-start | bytes 294920 | tf_op jit(solution)/shard_map/ppermute | solution.py:37
  137.9 3.1 %collective-permute-done.3 = bf16[384,128]{1,0:T(8,128)(2,1)S(1)} collective-permute-done((bf16[384,128]{1,0:T(8,128)(2,1)S(1)}, bf16[384,128]{1,0:T(8,128)(2,1)S(1)}, u32[]{:S(2)}, u32[]{:S(2)}) %collective-permute-start.3) | collective-permute-done | bytes 98336 | tf_op jit(solution)/shard_map/ppermute | solution.py:37
  141.0 14.7 %collective-permute-done.4 = bf16[384,128]{1,0:T(8,128)(2,1)S(1)} collective-permute-done((bf16[384,128]{1,0:T(8,128)(2,1)S(1)}, bf16[384,128]{1,0:T(8,128)(2,1)S(1)}, u32[]{:S(2)}, u32[]{:S(2)}) %collective-permute-start.4) | collective-permute-done | bytes 98336 | tf_op jit(solution)/shard_map/ppermute | solution.py:37
  155.7 0.8 all-to-all-done.1
  156.6 5.4 %collective-permute-start.5 = (bf16[256,128]{1,0:T(8,128)(2,1)S(1)}, bf16[256,128]{1,0:T(8,128)(2,1)S(1)}, u32[]{:S(2)}, u32[]{:S(2)}) collective-permute-start(bf16[256,128]{1,0:T(8,128)(2,1)S(1)} %get-tuple-element.20), channel_id=1, source_target_pairs={{0,0},{1,1},{2,32},{3,33},{4,64},{5,65},{6,96},{7,97},{8,8},{9,9},... | collective-permute-start | bytes 196616 | tf_op jit(solution)/shard_map/ppermute | solution.py:37
  162.0 6.0 %collective-permute-start.6 = (bf16[256,128]{1,0:T(8,128)(2,1)S(1)}, bf16[256,128]{1,0:T(8,128)(2,1)S(1)}, u32[]{:S(2)}, u32[]{:S(2)}) collective-permute-start(bf16[256,128]{1,0:T(8,128)(2,1)S(1)} %get-tuple-element.21), channel_id=1, source_target_pairs={{0,8},{1,9},{2,40},{3,41},{4,72},{5,73},{6,104},{7,105},{8,0},{9,1... | collective-permute-start | bytes 196616 | tf_op jit(solution)/shard_map/ppermute | solution.py:37
  168.0 0.7 pad_maximum_fusion.1
  168.7 4.0 %collective-permute-done.6 = bf16[256,128]{1,0:T(8,128)(2,1)S(1)} collective-permute-done((bf16[256,128]{1,0:T(8,128)(2,1)S(1)}, bf16[256,128]{1,0:T(8,128)(2,1)S(1)}, u32[]{:S(2)}, u32[]{:S(2)}) %collective-permute-start.6) | collective-permute-done | bytes 65568 | tf_op jit(solution)/shard_map/ppermute | solution.py:37
  172.7 0.7 subtract_convert_fusion
  (19 shorter events, 0.5 us)
Async XLA Ops:
  7.2 76.3 %all-gather.7.cloned.1.call-start = ((), (), s32[]{:S(2)}) async-start(), calls=%async_computation.2 | async-start | bytes 5308416 | tf_op jit(solution)/shard_map/all_gather | solution.py:74
  8.2 21.3 %collective-permute-start = (bf16[384,128]{1,0:T(8,128)(2,1)S(1)}, bf16[384,128]{1,0:T(8,128)(2,1)S(1)}, u32[]{:S(2)}, u32[]{:S(2)}) collective-permute-start(bf16[384,128]{1,0:T(8,128)(2,1)S(1)} %select_bitcast_fusion.4), channel_id=1, source_target_pairs={{0,8},{1,9},{2,10},{3,11},{4,12},{5,13},{6,14},{7,15},{8,0},{9,1},... | collective-permute-start | bytes 294920 | tf_op jit(solution)/shard_map/ppermute | solution.py:37
  29.5 86.7 %all-gather.9.cloned.1.call-start = ((), (), s32[]{:S(2)}) async-start(), calls=%async_computation.3 | async-start | bytes 3538944 | tf_op jit(solution)/shard_map/all_gather | solution.py:77
  31.6 10.5 %collective-permute-start.2 = (bf16[384,256]{1,0:T(8,128)(2,1)S(1)}, bf16[384,256]{1,0:T(8,128)(2,1)S(1)}, u32[]{:S(2)}, u32[]{:S(2)}) collective-permute-start(bf16[384,256]{1,0:T(8,128)(2,1)S(1)} %maximum_multiply_fusion), channel_id=1, source_target_pairs={{0,16},{1,17},{2,18},{3,19},{4,20},{5,21},{6,22},{7,23},{8,24},{9,... | collective-permute-start | bytes 589832 | tf_op jit(solution)/shard_map/ppermute | solution.py:37
  34.3 13.3 %collective-permute-start.1 = (bf16[384,256]{1,0:T(8,128)(2,1)S(1)}, bf16[384,256]{1,0:T(8,128)(2,1)S(1)}, u32[]{:S(2)}, u32[]{:S(2)}) collective-permute-start(bf16[384,256]{1,0:T(8,128)(2,1)S(1)} %maximum_multiply_fusion), channel_id=1, source_target_pairs={{0,0},{1,1},{2,32},{3,33},{4,64},{5,65},{6,96},{7,97},{8,8},{9,9},... | collective-permute-start | bytes 589832 | tf_op jit(solution)/shard_map/ppermute | solution.py:37
  88.2 14.4 %all-to-all-start = ((bf16[4,384,256]{2,1,0:T(8,128)(2,1)}), bf16[4,384,256]{2,1,0:T(8,128)(2,1)S(1)}, u32[]{:S(2)}, u32[]{:S(2)}) async-start(bf16[4,384,256]{2,1,0:T(8,128)(2,1)} %bitcast_convert_fusion), calls=%async_computation | async-start | bytes 1572864 | tf_op jit(solution)/shard_map/all_to_all | solution.py:81
  119.5 53.3 %copy-start = (bf16[2,256,128]{2,1,0:T(8,128)(2,1)S(1)}, bf16[2,256,128]{2,1,0:T(8,128)(2,1)}, u32[]{:S(2)}) copy-start(bf16[2,256,128]{2,1,0:T(8,128)(2,1)} %param.7) | copy-start | bytes 393220
  120.4 36.1 %all-to-all-start.1 = ((bf16[4,256,256]{2,1,0:T(8,128)(2,1)}), bf16[4,256,256]{2,1,0:T(8,128)(2,1)S(1)}, u32[]{:S(2)}, u32[]{:S(2)}) async-start(bf16[4,256,256]{2,1,0:T(8,128)(2,1)} %reverse_select_fusion), calls=%async_computation.1 | async-start | bytes 1048576 | tf_op jit(solution)/shard_map/all_to_all | solution.py:90
  128.7 12.3 %collective-permute-start.3 = (bf16[384,128]{1,0:T(8,128)(2,1)S(1)}, bf16[384,128]{1,0:T(8,128)(2,1)S(1)}, u32[]{:S(2)}, u32[]{:S(2)}) collective-permute-start(bf16[384,128]{1,0:T(8,128)(2,1)S(1)} %get-tuple-element.16), channel_id=1, source_target_pairs={{0,0},{1,1},{2,32},{3,33},{4,64},{5,65},{6,96},{7,97},{8,8},{9,9},... | collective-permute-start | bytes 294920 | tf_op jit(solution)/shard_map/ppermute | solution.py:37
  132.5 23.2 %collective-permute-start.4 = (bf16[384,128]{1,0:T(8,128)(2,1)S(1)}, bf16[384,128]{1,0:T(8,128)(2,1)S(1)}, u32[]{:S(2)}, u32[]{:S(2)}) collective-permute-start(bf16[384,128]{1,0:T(8,128)(2,1)S(1)} %get-tuple-element.17), channel_id=1, source_target_pairs={{0,8},{1,9},{2,40},{3,41},{4,72},{5,73},{6,104},{7,105},{8,0},{9,1... | collective-permute-start | bytes 294920 | tf_op jit(solution)/shard_map/ppermute | solution.py:37
  156.6 12.1 %collective-permute-start.5 = (bf16[256,128]{1,0:T(8,128)(2,1)S(1)}, bf16[256,128]{1,0:T(8,128)(2,1)S(1)}, u32[]{:S(2)}, u32[]{:S(2)}) collective-permute-start(bf16[256,128]{1,0:T(8,128)(2,1)S(1)} %get-tuple-element.20), channel_id=1, source_target_pairs={{0,0},{1,1},{2,32},{3,33},{4,64},{5,65},{6,96},{7,97},{8,8},{9,9},... | collective-permute-start | bytes 196616 | tf_op jit(solution)/shard_map/ppermute | solution.py:37
  162.0 10.7 %collective-permute-start.6 = (bf16[256,128]{1,0:T(8,128)(2,1)S(1)}, bf16[256,128]{1,0:T(8,128)(2,1)S(1)}, u32[]{:S(2)}, u32[]{:S(2)}) collective-permute-start(bf16[256,128]{1,0:T(8,128)(2,1)S(1)} %get-tuple-element.21), channel_id=1, source_target_pairs={{0,8},{1,9},{2,40},{3,41},{4,72},{5,73},{6,104},{7,105},{8,0},{9,1... | collective-permute-start | bytes 196616 | tf_op jit(solution)/shard_map/ppermute | solution.py:37
Sparse Core Ops, SparseCore 0:
  29.7 44.7 all-gather.6
  76.6 35.4 all-gather.8

commit v8 on v7

--- a/solution.py
+++ b/solution.py
@@ -78,7 +78,10 @@
     rows = lax.all_gather(turned, "zh")
 
     partial = panel_partial(block, rows)
-    parts = lax.all_to_all(partial, "x", split_axis=0, concat_axis=0, tiled=True)
+    partial = jnp.where(lax.axis_index("core") == 0, partial, partial[::-1])
+    parts = lax.all_to_all(
+        partial, ("x", "core"), split_axis=0, concat_axis=0, tiled=True, axis_index_groups=BOTH_WAYS
+    )
     weight = flags(x).astype(jnp.float32)
     panel = (-(jnp.sum(parts.astype(jnp.float32), axis=0) * weight)).astype(jnp.bfloat16)
     panel_rows = lax.all_gather(panel, "x")

time: 182 us -> 182 us (level)
  waiting for transfers between devices: 39.7 us -> 37.5 us
  starting transfers between devices: 44.9 us -> 46.8 us
  transfers between devices with their start and end apart: 11 -> 11, of which waited for: 7 -> 6; matrix products, arithmetic and copies ran while one was open for 5% -> 5% of each run, Pallas kernels for 0% -> 0%
where the time goes in v8:
time: 182 us; the launch traced here: 180 us
  blocking collectives  66.7 us (37%)
  starting transfers between devices  46.8 us (26%)
  waiting for transfers between devices  37.5 us (21%)
  between operations  14.2 us (8%)
  other arithmetic  7.55 us (4%)
  matrix products  7.01 us (4%)
    all_gather x1, blocking collectives, on_device(): rows = lax.all_gather(turned, 'zh')  35.9 us
    ppermute x7, starting transfers between devices, move(): return lax.ppermute(value, AXES, listed)  33 us
    ppermute x7, waiting for transfers between devices, move(): return lax.ppermute(value, AXES, listed)  28.9 us
    all_gather x1, blocking collectives, on_device(): block_parts = lax.all_gather(inverse_block.T, 'zl')  17.5 us
    all_gather x1, blocking collectives, on_device(): panel_rows = lax.all_gather(panel, 'x')  13.3 us
    all_to_all x1, starting transfers between devices, on_device(): lax.all_to_all(shares, ('zh', 'core'), split_axis=0, concat_axis=0, tiled...  8.96 us
    all_to_all x1, waiting for transfers between devices, on_device(): lax.all_to_all(partial, ('x', 'core'), split_axis=0, concat_axis=0, tiled...  8.59 us
    all_to_all x1, starting transfers between devices, on_device(): lax.all_to_all(partial, ('x', 'core'), split_axis=0, concat_axis=0, tiled...  4.8 us
  transfers between devices with their start and end apart: 11, of which 6 were waited for; matrix products, arithmetic and copies ran while one was open for 5% of the time, Pallas kernels for 0%

profile of v8, /device:TPU:6, one launch (start us, length us, event | category | flops | bytes accessed | tf_op | source)
XLA Modules:
  0.0 180.1 jit_solution(2874753967407535105)
XLA Ops:
  7.2 1.0 select_bitcast_fusion.4
  8.2 3.8 %collective-permute-start = (bf16[384,128]{1,0:T(8,128)(2,1)S(1)}, bf16[384,128]{1,0:T(8,128)(2,1)S(1)}, u32[]{:S(2)}, u32[]{:S(2)}) collective-permute-start(bf16[384,128]{1,0:T(8,128)(2,1)S(1)} %select_bitcast_fusion.4), channel_id=1, source_target_pairs={{0,8},{1,9},{2,10},{3,11},{4,12},{5,13},{6,14},{7,15},{8,0},{9,1},... | collective-permute-start | bytes 294920 | tf_op jit(solution)/shard_map/ppermute | solution.py:37
  12.0 17.5 %all-gather = bf16[768,384]{1,0:T(8,128)(2,1)} all-gather(bf16[192,384]{1,0:T(8,128)(2,1)} %bitcast.73), channel_id=2, replica_groups=mesh['zh'=4,'y'=4,'zl'=4,'x'=4,'core'=2] {'zl'}, dimensions={0}, use_global_device_ids=true | all-gather | bytes 737280 | tf_op jit(solution)/shard_map/all_gather | solution.py:68
  29.6 0.8 convert_bitcast_fusion
  30.5 1.0 bitcast_select_fusion.1
  31.5 0.1 maximum_multiply_fusion
  31.6 2.7 %collective-permute-start.2 = (bf16[384,256]{1,0:T(8,128)(2,1)S(1)}, bf16[384,256]{1,0:T(8,128)(2,1)S(1)}, u32[]{:S(2)}, u32[]{:S(2)}) collective-permute-start(bf16[384,256]{1,0:T(8,128)(2,1)S(1)} %maximum_multiply_fusion), channel_id=1, source_target_pairs={{0,16},{1,17},{2,18},{3,19},{4,20},{5,21},{6,22},{7,23},{8,24},{9,... | collective-permute-start | bytes 589832 | tf_op jit(solution)/shard_map/ppermute | solution.py:37
  34.3 4.8 %collective-permute-start.1 = (bf16[384,256]{1,0:T(8,128)(2,1)S(1)}, bf16[384,256]{1,0:T(8,128)(2,1)S(1)}, u32[]{:S(2)}, u32[]{:S(2)}) collective-permute-start(bf16[384,256]{1,0:T(8,128)(2,1)S(1)} %maximum_multiply_fusion), channel_id=1, source_target_pairs={{0,0},{1,1},{2,32},{3,33},{4,64},{5,65},{6,96},{7,97},{8,8},{9,9},... | collective-permute-start | bytes 589832 | tf_op jit(solution)/shard_map/ppermute | solution.py:37
  39.1 2.9 %collective-permute-done.2 = bf16[384,256]{1,0:T(8,128)(2,1)S(1)} collective-permute-done((bf16[384,256]{1,0:T(8,128)(2,1)S(1)}, bf16[384,256]{1,0:T(8,128)(2,1)S(1)}, u32[]{:S(2)}, u32[]{:S(2)}) %collective-permute-start.2) | collective-permute-done | bytes 196640 | tf_op jit(solution)/shard_map/ppermute | solution.py:37
  42.1 0.8 pad_maximum_fusion
  42.9 4.6 %collective-permute-done.1 = bf16[384,256]{1,0:T(8,128)(2,1)S(1)} collective-permute-done((bf16[384,256]{1,0:T(8,128)(2,1)S(1)}, bf16[384,256]{1,0:T(8,128)(2,1)S(1)}, u32[]{:S(2)}, u32[]{:S(2)}) %collective-permute-start.1) | collective-permute-done | bytes 196640 | tf_op jit(solution)/shard_map/ppermute | solution.py:37
  47.6 35.9 %all-gather.2 = bf16[1536,256]{1,0:T(8,128)(2,1)S(1)} all-gather(bf16[384,256]{1,0:T(8,128)(2,1)S(1)} %collective-permute-done.1), channel_id=4, replica_groups=mesh['zh'=4,'y'=4,'zl'=4,'x'=4,'core'=2] {'zh'}, dimensions={0}, use_global_device_ids=true | all-gather | bytes 983040 | tf_op jit(solution)/shard_map/all_gather | solution.py:78
  83.5 3.8 %bitcast_convert_fusion = bf16[4,384,256]{2,1,0:T(8,128)(2,1)S(1)} fusion(bf16[4,2,4,192,384]{4,3,2,1,0:T(8,128)(2,1)} %bitcast.74, bf16[4,2,192,256,1]{3,2,1,0,4:T(8,128)(2,1)S(1)} %bitcast.71), kind=kOutput, calls=%fused_computation | convolution fusion | flops 1208352768 | bytes 6291456 | tf_op jit(solution)/shard_map/ycztS,zctj->ySj/dot_general | solution.py:42
  87.3 1.0 reverse_select_fusion
  88.3 4.8 %all-to-all-start = ((bf16[4,384,256]{2,1,0:T(8,128)(2,1)}), bf16[4,384,256]{2,1,0:T(8,128)(2,1)S(1)}, u32[]{:S(2)}, u32[]{:S(2)}) async-start(bf16[4,384,256]{2,1,0:T(8,128)(2,1)} %reverse_select_fusion), calls=%async_computation | async-start | bytes 1572864 | tf_op jit(solution)/shard_map/all_to_all | solution.py:82
  93.2 8.6 %all-to-all-done = bf16[4,384,256]{2,1,0:T(8,128)(2,1)S(1)} async-done(((bf16[4,384,256]{2,1,0:T(8,128)(2,1)}), bf16[4,384,256]{2,1,0:T(8,128)(2,1)S(1)}, u32[]{:S(2)}, u32[]{:S(2)}) %all-to-all-start) | async-done | bytes 786464 | tf_op jit(solution)/shard_map/all_to_all | solution.py:82
  101.8 0.1 convert_reduce_fusion
  101.9 0.1 fusion.5
  102.0 13.3 %all_gather.34 = bf16[4,384,256]{2,1,0:T(8,128)(2,1)S(1)} all-gather(bf16[1,384,256]{2,1,0:T(8,128)(2,1)S(1)} %fusion.5), channel_id=1, replica_groups=mesh['zh'=4,'y'=4,'zl'=4,'x'=4,'core'=2] {'x'}, dimensions={0}, use_global_device_ids=true | all-gather | bytes 983040 | tf_op jit(solution)/shard_map/all_gather | solution.py:87
  115.3 3.2 %fusion = bf16[256,2,2,256]{0,3,2,1:T(8,128)(2,1)S(1)} fusion(bf16[4,2,2,384,256]{4,3,2,1,0:T(8,128)(2,1)} %bitcast.75, bf16[4,384,256]{2,1,0:T(8,128)(2,1)S(1)} %all_gather.34), kind=kOutput, calls=%fused_computation.3 | convolution fusion | flops 805568512 | bytes 4456448 | tf_op jit(solution)/shard_map/gcpsi,gsj->pcij/dot_general | solution.py:47
  118.6 0.9 reverse_select_fusion.1
  119.5 9.0 %all-to-all-start.1 = ((bf16[4,256,256]{2,1,0:T(8,128)(2,1)}), bf16[4,256,256]{2,1,0:T(8,128)(2,1)S(1)}, u32[]{:S(2)}, u32[]{:S(2)}) async-start(bf16[4,256,256]{2,1,0:T(8,128)(2,1)} %reverse_select_fusion.1), calls=%async_computation.1 | async-start | bytes 1048576 | tf_op jit(solution)/shard_map/all_to_all | solution.py:93
  128.5 0.1 negate_convert_fusion
  128.7 3.5 %collective-permute-start.3 = (bf16[384,128]{1,0:T(8,128)(2,1)S(1)}, bf16[384,128]{1,0:T(8,128)(2,1)S(1)}, u32[]{:S(2)}, u32[]{:S(2)}) collective-permute-start(bf16[384,128]{1,0:T(8,128)(2,1)S(1)} %get-tuple-element.16), channel_id=1, source_target_pairs={{0,0},{1,1},{2,32},{3,33},{4,64},{5,65},{6,96},{7,97},{8,8},{9,9},... | collective-permute-start | bytes 294920 | tf_op jit(solution)/shard_map/ppermute | solution.py:37
  132.1 6.1 %collective-permute-start.4 = (bf16[384,128]{1,0:T(8,128)(2,1)S(1)}, bf16[384,128]{1,0:T(8,128)(2,1)S(1)}, u32[]{:S(2)}, u32[]{:S(2)}) collective-permute-start(bf16[384,128]{1,0:T(8,128)(2,1)S(1)} %get-tuple-element.17), channel_id=1, source_target_pairs={{0,8},{1,9},{2,40},{3,41},{4,72},{5,73},{6,104},{7,105},{8,0},{9,1... | collective-permute-start | bytes 294920 | tf_op jit(solution)/shard_map/ppermute | solution.py:37
  138.2 2.7 %collective-permute-done.3 = bf16[384,128]{1,0:T(8,128)(2,1)S(1)} collective-permute-done((bf16[384,128]{1,0:T(8,128)(2,1)S(1)}, bf16[384,128]{1,0:T(8,128)(2,1)S(1)}, u32[]{:S(2)}, u32[]{:S(2)}) %collective-permute-start.3) | collective-permute-done | bytes 98336 | tf_op jit(solution)/shard_map/ppermute | solution.py:37
  140.9 14.7 %collective-permute-done.4 = bf16[384,128]{1,0:T(8,128)(2,1)S(1)} collective-permute-done((bf16[384,128]{1,0:T(8,128)(2,1)S(1)}, bf16[384,128]{1,0:T(8,128)(2,1)S(1)}, u32[]{:S(2)}, u32[]{:S(2)}) %collective-permute-start.4) | collective-permute-done | bytes 98336 | tf_op jit(solution)/shard_map/ppermute | solution.py:37
  155.8 6.1 %collective-permute-start.5 = (bf16[256,128]{1,0:T(8,128)(2,1)S(1)}, bf16[256,128]{1,0:T(8,128)(2,1)S(1)}, u32[]{:S(2)}, u32[]{:S(2)}) collective-permute-start(bf16[256,128]{1,0:T(8,128)(2,1)S(1)} %get-tuple-element.20), channel_id=1, source_target_pairs={{0,0},{1,1},{2,32},{3,33},{4,64},{5,65},{6,96},{7,97},{8,8},{9,9},... | collective-permute-start | bytes 196616 | tf_op jit(solution)/shard_map/ppermute | solution.py:37
  161.9 6.0 %collective-permute-start.6 = (bf16[256,128]{1,0:T(8,128)(2,1)S(1)}, bf16[256,128]{1,0:T(8,128)(2,1)S(1)}, u32[]{:S(2)}, u32[]{:S(2)}) collective-permute-start(bf16[256,128]{1,0:T(8,128)(2,1)S(1)} %get-tuple-element.21), channel_id=1, source_target_pairs={{0,8},{1,9},{2,40},{3,41},{4,72},{5,73},{6,104},{7,105},{8,0},{9,1... | collective-permute-start | bytes 196616 | tf_op jit(solution)/shard_map/ppermute | solution.py:37
  167.9 0.7 pad_maximum_fusion.1
  168.6 3.9 %collective-permute-done.6 = bf16[256,128]{1,0:T(8,128)(2,1)S(1)} collective-permute-done((bf16[256,128]{1,0:T(8,128)(2,1)S(1)}, bf16[256,128]{1,0:T(8,128)(2,1)S(1)}, u32[]{:S(2)}, u32[]{:S(2)}) %collective-permute-start.6) | collective-permute-done | bytes 65568 | tf_op jit(solution)/shard_map/ppermute | solution.py:37
  172.5 0.7 subtract_convert_fusion
  (20 shorter events, 0.5 us)
Async XLA Ops:
  7.2 76.4 %all-gather.7.cloned.1.call-start = ((), (), s32[]{:S(2)}) async-start(), calls=%async_computation.2 | async-start | bytes 5308416 | tf_op jit(solution)/shard_map/all_gather | solution.py:74
  8.2 21.3 %collective-permute-start = (bf16[384,128]{1,0:T(8,128)(2,1)S(1)}, bf16[384,128]{1,0:T(8,128)(2,1)S(1)}, u32[]{:S(2)}, u32[]{:S(2)}) collective-permute-start(bf16[384,128]{1,0:T(8,128)(2,1)S(1)} %select_bitcast_fusion.4), channel_id=1, source_target_pairs={{0,8},{1,9},{2,10},{3,11},{4,12},{5,13},{6,14},{7,15},{8,0},{9,1},... | collective-permute-start | bytes 294920 | tf_op jit(solution)/shard_map/ppermute | solution.py:37
  29.5 85.8 %all-gather.9.cloned.1.call-start = ((), (), s32[]{:S(2)}) async-start(), calls=%async_computation.3 | async-start | bytes 3538944 | tf_op jit(solution)/shard_map/all_gather | solution.py:77
  31.6 10.5 %collective-permute-start.2 = (bf16[384,256]{1,0:T(8,128)(2,1)S(1)}, bf16[384,256]{1,0:T(8,128)(2,1)S(1)}, u32[]{:S(2)}, u32[]{:S(2)}) collective-permute-start(bf16[384,256]{1,0:T(8,128)(2,1)S(1)} %maximum_multiply_fusion), channel_id=1, source_target_pairs={{0,16},{1,17},{2,18},{3,19},{4,20},{5,21},{6,22},{7,23},{8,24},{9,... | collective-permute-start | bytes 589832 | tf_op jit(solution)/shard_map/ppermute | solution.py:37
  34.3 13.3 %collective-permute-start.1 = (bf16[384,256]{1,0:T(8,128)(2,1)S(1)}, bf16[384,256]{1,0:T(8,128)(2,1)S(1)}, u32[]{:S(2)}, u32[]{:S(2)}) collective-permute-start(bf16[384,256]{1,0:T(8,128)(2,1)S(1)} %maximum_multiply_fusion), channel_id=1, source_target_pairs={{0,0},{1,1},{2,32},{3,33},{4,64},{5,65},{6,96},{7,97},{8,8},{9,9},... | collective-permute-start | bytes 589832 | tf_op jit(solution)/shard_map/ppermute | solution.py:37
  88.3 13.5 %all-to-all-start = ((bf16[4,384,256]{2,1,0:T(8,128)(2,1)}), bf16[4,384,256]{2,1,0:T(8,128)(2,1)S(1)}, u32[]{:S(2)}, u32[]{:S(2)}) async-start(bf16[4,384,256]{2,1,0:T(8,128)(2,1)} %reverse_select_fusion), calls=%async_computation | async-start | bytes 1572864 | tf_op jit(solution)/shard_map/all_to_all | solution.py:82
  118.6 54.0 %copy-start = (bf16[2,256,128]{2,1,0:T(8,128)(2,1)S(1)}, bf16[2,256,128]{2,1,0:T(8,128)(2,1)}, u32[]{:S(2)}) copy-start(bf16[2,256,128]{2,1,0:T(8,128)(2,1)} %param.7) | copy-start | bytes 393220
  119.5 36.1 %all-to-all-start.1 = ((bf16[4,256,256]{2,1,0:T(8,128)(2,1)}), bf16[4,256,256]{2,1,0:T(8,128)(2,1)S(1)}, u32[]{:S(2)}, u32[]{:S(2)}) async-start(bf16[4,256,256]{2,1,0:T(8,128)(2,1)} %reverse_select_fusion.1), calls=%async_computation.1 | async-start | bytes 1048576 | tf_op jit(solution)/shard_map/all_to_all | solution.py:93
  128.7 12.3 %collective-permute-start.3 = (bf16[384,128]{1,0:T(8,128)(2,1)S(1)}, bf16[384,128]{1,0:T(8,128)(2,1)S(1)}, u32[]{:S(2)}, u32[]{:S(2)}) collective-permute-start(bf16[384,128]{1,0:T(8,128)(2,1)S(1)} %get-tuple-element.16), channel_id=1, source_target_pairs={{0,0},{1,1},{2,32},{3,33},{4,64},{5,65},{6,96},{7,97},{8,8},{9,9},... | collective-permute-start | bytes 294920 | tf_op jit(solution)/shard_map/ppermute | solution.py:37
  132.1 23.5 %collective-permute-start.4 = (bf16[384,128]{1,0:T(8,128)(2,1)S(1)}, bf16[384,128]{1,0:T(8,128)(2,1)S(1)}, u32[]{:S(2)}, u32[]{:S(2)}) collective-permute-start(bf16[384,128]{1,0:T(8,128)(2,1)S(1)} %get-tuple-element.17), channel_id=1, source_target_pairs={{0,8},{1,9},{2,40},{3,41},{4,72},{5,73},{6,104},{7,105},{8,0},{9,1... | collective-permute-start | bytes 294920 | tf_op jit(solution)/shard_map/ppermute | solution.py:37
  155.8 12.8 %collective-permute-start.5 = (bf16[256,128]{1,0:T(8,128)(2,1)S(1)}, bf16[256,128]{1,0:T(8,128)(2,1)S(1)}, u32[]{:S(2)}, u32[]{:S(2)}) collective-permute-start(bf16[256,128]{1,0:T(8,128)(2,1)S(1)} %get-tuple-element.20), channel_id=1, source_target_pairs={{0,0},{1,1},{2,32},{3,33},{4,64},{5,65},{6,96},{7,97},{8,8},{9,9},... | collective-permute-start | bytes 196616 | tf_op jit(solution)/shard_map/ppermute | solution.py:37
  161.9 10.6 %collective-permute-start.6 = (bf16[256,128]{1,0:T(8,128)(2,1)S(1)}, bf16[256,128]{1,0:T(8,128)(2,1)S(1)}, u32[]{:S(2)}, u32[]{:S(2)}) collective-permute-start(bf16[256,128]{1,0:T(8,128)(2,1)S(1)} %get-tuple-element.21), channel_id=1, source_target_pairs={{0,8},{1,9},{2,40},{3,41},{4,72},{5,73},{6,104},{7,105},{8,0},{9,1... | collective-permute-start | bytes 196616 | tf_op jit(solution)/shard_map/ppermute | solution.py:37
Sparse Core Ops, SparseCore 0:
  29.7 44.7 all-gather.6
  76.6 35.4 all-gather.8
